TPU v7x, 32 devices: a whole 2x2x4 slice. The times are simulated.
32 devices in a mesh: shard: 2 (over x), rep: 16 (over z, y, core).
Axes of the slice: x: 2, y: 2, z: 4, core: 2. Of those that a mesh axis runs over, the one named last changes fastest.
Arguments:
- tokens: bfloat16 [16384, 1024], P(('shard', 'rep')), may hold values from -6 to 6
- routes: int32 [16384, 8], P(('shard', 'rep')), may hold values from 0 to 15, all different within a row; in each aligned block of 512 rows (0 to 511, 512 to 1023, ...) at most 288 rows name the same one
- out_grad: bfloat16 [16384, 1024], P(('shard', 'rep')), may hold values from -6 to 6
- query_weight: bfloat16 [1024, 1024], P('shard'), may hold values from -0.625 to 0.625
- key_weight: bfloat16 [1024, 512], P('shard'), may hold values from -0.625 to 0.625
- value_weight: bfloat16 [1024, 512], P('shard'), may hold values from -0.1875 to 0.1875
- output_weight: bfloat16 [1024, 1024], P('shard'), may hold values from -4 to 4
- norm_one: bfloat16 [1024], P('shard'), may hold values from 0.5 to 1.5
- norm_two: bfloat16 [1024], P('shard'), may hold values from 0.5 to 1.5
- router_weight: bfloat16 [1024, 16], P('shard'), may hold values from -0.09375 to 0.09375
- expert_in: bfloat16 [16, 2, 1024, 512], P('shard'), may hold values from -0.1875 to 0.1875
- expert_out: bfloat16 [16, 1024, 512], P('shard'), may hold values from -4 to 4
Outputs:
- layer_out: bfloat16 [16384, 1024], P(('shard', 'rep'))
- tokens_grad: float32 [16384, 1024], P(('shard', 'rep'))
- query_grad: float32 [1024, 1024], P('shard')
- key_grad: float32 [1024, 512], P('shard')
- value_grad: float32 [1024, 512], P('shard')
- output_grad: float32 [1024, 1024], P('shard')
- norm_one_grad: float32 [1024], P('shard')
- norm_two_grad: float32 [1024], P('shard')
- router_grad: float32 [1024, 16], P('shard')
- expert_in_grad: float32 [16, 2, 1024, 512], P('shard')
- expert_out_grad: float32 [16, 1024, 512], P('shard')
Inputs may be any that keep to these rules, and one draw needn't show every extreme that they name: `routes`: each row names 8 different experts. Among the 512 rows of one device no expert is named more than 288 times, and in every draw some expert is named exactly 288 times in some device's rows.
All inputs are finite; a program needn't handle non-finite values.
Results may differ from a plain program's by a relative error of at most 0.02.
Values may be sent and summed in bfloat16 or wider, within the bound.
A program may use at most 448 MiB of HBM per device.

v0:
```python
import jax
import jax.numpy as jnp
from jax import lax
from jax.sharding import PartitionSpec as P

D = 1024
HEADS = 16
KV_HEADS = 8
HEAD_DIM = 64
EXPERTS = 16
SEQ = 512
CAP = 288


EPSILON = 1e-06
ATTN_SCALE = 0.015625
RESIDUAL_SCALE = 0.22
ROPE_BASE = 10000.0


def rope_tables(length, width):
    half_width = width // 2
    frequency = ROPE_BASE ** (-2.0 * jnp.arange(half_width, dtype=jnp.float32) / width)
    angles = jnp.arange(length, dtype=jnp.float32)[:, None] * frequency[None, :]
    return (jnp.cos(angles)[:, None, :], jnp.sin(angles)[:, None, :])


def rotate(values, cosine, sine_part):
    half_width = values.shape[-1] // 2
    first_half = values[..., :half_width]
    second_half = values[..., half_width:]
    return jnp.concatenate(
        [
            first_half * cosine - second_half * sine_part,
            second_half * cosine + first_half * sine_part,
        ],
        -1,
    )


def unrotate(values, cosine, sine_part):
    half_width = values.shape[-1] // 2
    first_half = values[..., :half_width]
    second_half = values[..., half_width:]
    return jnp.concatenate(
        [
            first_half * cosine + second_half * sine_part,
            second_half * cosine - first_half * sine_part,
        ],
        -1,
    )


def dispatch(routes):
    token_count = routes.shape[0]
    experts_iota = jnp.arange(EXPERTS, dtype=jnp.int32)
    onehot = (routes[:, :, None] == experts_iota[None, None, :]).astype(jnp.int32)
    chosen_any = jnp.sum(onehot, 1)
    slot_ranks = jnp.cumsum(chosen_any, 0) - chosen_any
    slot_place = jnp.sum(onehot * slot_ranks[:, None, :], 2)
    slot_of = routes * CAP + slot_place
    sources = jnp.broadcast_to(jnp.arange(token_count, dtype=jnp.int32)[:, None], routes.shape)
    token_of = (
        jnp.full((EXPERTS * CAP,), token_count, jnp.int32)
        .at[slot_of.reshape(-1)]
        .set(sources.reshape(-1))
    )
    return (onehot, slot_of, token_of)


def block_scores(query_block, key_block, first_row):
    scores = ATTN_SCALE * jnp.einsum(
        "sqgjd,skgd->sgjqk", query_block, key_block, preferred_element_type=jnp.float32
    )
    query_pos = first_row + jnp.arange(query_block.shape[1])
    key_pos = jnp.arange(key_block.shape[1])
    return jnp.where(query_pos[:, None] >= key_pos[None, :], scores, -jnp.inf)


def expert_forward(expert_rows, gate_up, down_proj):
    pre_act = jnp.einsum("ecd,etdf->tecf", expert_rows, gate_up, preferred_element_type=jnp.float32)
    hidden = (jax.nn.silu(pre_act[0]) * pre_act[1]).astype(jnp.bfloat16)
    result = jnp.einsum("ecf,edf->ecd", hidden, down_proj, preferred_element_type=jnp.float32)
    return (pre_act, result)


def expert_backward(pre_all, slot_grads, gate_up, down_proj):
    hidden_grad = jnp.einsum(
        "ecd,edf->ecf", slot_grads, down_proj, preferred_element_type=jnp.float32
    )
    sigmoid_gate = jax.nn.sigmoid(pre_all[0])
    gate_grad = hidden_grad * pre_all[1] * sigmoid_gate * (1.0 + pre_all[0] * (1.0 - sigmoid_gate))
    up_grad = hidden_grad * (pre_all[0] * sigmoid_gate)
    pair_grad = jnp.stack([gate_grad, up_grad]).astype(jnp.bfloat16)
    input_grad = jnp.einsum(
        "tecf,etdf->ecd", pair_grad, gate_up, preferred_element_type=jnp.float32
    )
    return (pair_grad, input_grad)


def expert_weight_term(expert_rows, pre_all, pair_all, slot_grads):
    hidden = (jax.nn.silu(pre_all[0]) * pre_all[1]).astype(jnp.bfloat16)
    in_term = jnp.einsum(
        "ecd,tecf->etdf", expert_rows, pair_all, preferred_element_type=jnp.float32
    )
    out_term = jnp.einsum("ecd,ecf->edf", slot_grads, hidden, preferred_element_type=jnp.float32)
    return jnp.concatenate([in_term, out_term[:, None]], 1)


def per_device(
    tokens,
    routes,
    out_grad,
    query_weight,
    key_weight,
    value_weight,
    output_weight,
    norm_one,
    norm_two,
    router_weight,
    expert_in,
    expert_out,
):
    row_count = tokens.shape[0]
    seq_count = row_count // SEQ
    group_heads = HEADS // KV_HEADS
    query_width = HEADS * HEAD_DIM
    block_rows = min(512, SEQ)
    attn_full = (
        lax.all_gather(query_weight, "shard", axis=0, tiled=True),
        lax.all_gather(key_weight, "shard", axis=0, tiled=True),
        lax.all_gather(value_weight, "shard", axis=0, tiled=True),
        lax.all_gather(output_weight, "shard", axis=0, tiled=True),
        lax.all_gather(norm_one, "shard", axis=0, tiled=True),
        lax.all_gather(norm_two, "shard", axis=0, tiled=True),
        lax.all_gather(router_weight, "shard", axis=0, tiled=True),
    )
    inputs_f = tokens.astype(jnp.float32)
    scale_one = lax.rsqrt(jnp.mean(inputs_f * inputs_f, -1, keepdims=True) + EPSILON)
    gain_one = attn_full[4].astype(jnp.float32)
    normed_one = (inputs_f * scale_one * gain_one).astype(jnp.bfloat16)
    query_pre = jnp.dot(normed_one, attn_full[0], preferred_element_type=jnp.float32)
    key_pre = jnp.dot(normed_one, attn_full[1], preferred_element_type=jnp.float32)
    value_low = jnp.dot(normed_one, attn_full[2], preferred_element_type=jnp.float32).astype(
        jnp.bfloat16
    )
    value_low = value_low.reshape(seq_count, SEQ, KV_HEADS, HEAD_DIM)
    cosine, sine_part = rope_tables(SEQ, HEAD_DIM)
    queries = rotate(query_pre.reshape(seq_count, SEQ, HEADS, HEAD_DIM), cosine, sine_part).astype(
        jnp.bfloat16
    )
    queries = queries.reshape(seq_count, SEQ, KV_HEADS, group_heads, HEAD_DIM)
    keys_low = rotate(
        key_pre.reshape(seq_count, SEQ, KV_HEADS, HEAD_DIM), cosine, sine_part
    ).astype(jnp.bfloat16)
    block_index = 0
    first_row = block_index * block_rows
    scores = block_scores(queries, keys_low, first_row)
    row_max = jnp.max(scores, -1, keepdims=True)
    exp_scores = jnp.exp(scores - row_max)
    row_total = jnp.sum(exp_scores, -1, keepdims=True)
    prob_low = (exp_scores / row_total).astype(jnp.bfloat16)
    head_outputs = jnp.einsum(
        "sgjqk,skgd->sqgjd", prob_low, value_low, preferred_element_type=jnp.float32
    )
    log_totals = [row_max + jnp.log(row_total)]
    attended = head_outputs.reshape(row_count, query_width).astype(jnp.bfloat16)
    branch = jnp.dot(attended, attn_full[3], preferred_element_type=jnp.float32)
    residual = inputs_f + RESIDUAL_SCALE * branch
    scale_two = lax.rsqrt(jnp.mean(residual * residual, -1, keepdims=True) + EPSILON)
    gain_two = attn_full[5].astype(jnp.float32)
    normed_two = (residual * scale_two * gain_two).astype(jnp.bfloat16)
    logits = jnp.dot(normed_two, attn_full[6], preferred_element_type=jnp.float32)
    onehot, slot_of, token_of = dispatch(routes)
    onehot_f = onehot.astype(jnp.float32)
    chosen = jnp.sum(onehot_f * logits[:, None, :], -1)
    gate_weights = jax.nn.softmax(chosen, -1)
    padded = jnp.concatenate([normed_two, jnp.zeros((1, D), jnp.bfloat16)], 0)
    expert_rows = padded[token_of].reshape(EXPERTS, CAP, D)
    piece_pair = (
        lax.all_gather(expert_in, "shard", axis=0, tiled=True),
        lax.all_gather(expert_out, "shard", axis=0, tiled=True),
    )
    pre_act, result = expert_forward(expert_rows, piece_pair[0], piece_pair[1])
    slot_values = result.reshape(EXPERTS * CAP, D)[slot_of]
    expert_mix = jnp.sum(gate_weights[:, :, None] * slot_values, 1)
    layer_out = (residual + RESIDUAL_SCALE * expert_mix).astype(jnp.bfloat16)
    grad_out = out_grad.astype(jnp.float32)
    mix_grad = RESIDUAL_SCALE * grad_out
    gate_grad = jnp.sum(slot_values * mix_grad[:, None, :], -1)
    chosen_grad = gate_weights * (gate_grad - jnp.sum(gate_weights * gate_grad, -1, keepdims=True))
    logit_grad = jnp.sum(onehot_f * chosen_grad[:, :, None], 1)
    gate_of_slot = (
        jnp.zeros((EXPERTS * CAP,), jnp.float32)
        .at[slot_of.reshape(-1)]
        .set(gate_weights.reshape(-1))
    )
    padded_grad = jnp.concatenate([mix_grad, jnp.zeros((1, D), jnp.float32)], 0)
    slot_grads = (
        (gate_of_slot[:, None] * padded_grad[token_of])
        .astype(jnp.bfloat16)
        .reshape(EXPERTS, CAP, D)
    )
    attn_back = (
        lax.all_gather(query_weight, "shard", axis=0, tiled=True),
        lax.all_gather(key_weight, "shard", axis=0, tiled=True),
        lax.all_gather(value_weight, "shard", axis=0, tiled=True),
        lax.all_gather(output_weight, "shard", axis=0, tiled=True),
        lax.all_gather(norm_one, "shard", axis=0, tiled=True),
        lax.all_gather(norm_two, "shard", axis=0, tiled=True),
        lax.all_gather(router_weight, "shard", axis=0, tiled=True),
    )
    piece_pair = (
        lax.all_gather(expert_in, "shard", axis=0, tiled=True),
        lax.all_gather(expert_out, "shard", axis=0, tiled=True),
    )
    pair_grad, input_grad = expert_backward(pre_act, slot_grads, piece_pair[0], piece_pair[1])
    exact = lax.Precision.HIGHEST
    router_f = attn_back[6].astype(jnp.float32)
    norm_grad_two = jnp.sum(input_grad.reshape(EXPERTS * CAP, D)[slot_of], 1) + jnp.dot(
        logit_grad, router_f.T, precision=exact
    )
    router_term = jnp.dot(normed_two.astype(jnp.float32).T, logit_grad, precision=exact)
    weighted_two = gain_two * norm_grad_two
    gain_two_term = jnp.sum(norm_grad_two * residual * scale_two, 0)
    residual_grad = (
        grad_out
        + scale_two * weighted_two
        - residual * scale_two**3 * jnp.mean(weighted_two * residual, -1, keepdims=True)
    )
    branch_grad = (RESIDUAL_SCALE * residual_grad).astype(jnp.bfloat16)
    output_term = jnp.einsum("tq,td->qd", attended, branch_grad, preferred_element_type=jnp.float32)
    attended_grad = jnp.einsum(
        "td,qd->tq", branch_grad, attn_back[3], preferred_element_type=jnp.float32
    ).astype(jnp.bfloat16)
    attended_grad = attended_grad.reshape(seq_count, SEQ, KV_HEADS, group_heads, HEAD_DIM)
    key_accum = jnp.zeros((seq_count, SEQ, KV_HEADS, HEAD_DIM), jnp.float32)
    value_accum = jnp.zeros((seq_count, SEQ, KV_HEADS, HEAD_DIM), jnp.float32)
    block_index = 0
    first_row = block_index * block_rows
    last_row = first_row + block_rows
    scores = block_scores(queries, keys_low, first_row)
    probs_f = jnp.exp(scores - log_totals[block_index])
    prob_low = probs_f.astype(jnp.bfloat16)
    value_accum = value_accum.at[:, :last_row].add(
        jnp.einsum("sgjqk,sqgjd->skgd", prob_low, attended_grad, preferred_element_type=jnp.float32)
    )
    prob_grad = jnp.einsum(
        "sqgjd,skgd->sgjqk", attended_grad, value_low, preferred_element_type=jnp.float32
    )
    score_grad = (probs_f * (prob_grad - jnp.sum(probs_f * prob_grad, -1, keepdims=True))).astype(
        jnp.bfloat16
    )
    query_blocks = ATTN_SCALE * jnp.einsum(
        "sgjqk,skgd->sqgjd", score_grad, keys_low, preferred_element_type=jnp.float32
    )
    key_accum = key_accum.at[:, :last_row].add(
        ATTN_SCALE
        * jnp.einsum("sgjqk,sqgjd->skgd", score_grad, queries, preferred_element_type=jnp.float32)
    )
    query_low = unrotate(query_blocks.reshape(seq_count, SEQ, HEADS, HEAD_DIM), cosine, sine_part)
    query_low = query_low.reshape(row_count, query_width).astype(jnp.bfloat16)
    key_low_grad = (
        unrotate(key_accum, cosine, sine_part)
        .reshape(row_count, KV_HEADS * HEAD_DIM)
        .astype(jnp.bfloat16)
    )
    value_low_grad = value_accum.reshape(row_count, KV_HEADS * HEAD_DIM).astype(jnp.bfloat16)
    query_term = jnp.einsum("td,tq->dq", normed_one, query_low, preferred_element_type=jnp.float32)
    key_term = jnp.einsum("td,tq->dq", normed_one, key_low_grad, preferred_element_type=jnp.float32)
    value_term = jnp.einsum(
        "td,tq->dq", normed_one, value_low_grad, preferred_element_type=jnp.float32
    )
    norm_grad_one = jnp.einsum(
        "tq,dq->td", query_low, attn_back[0], preferred_element_type=jnp.float32
    )
    norm_grad_one = norm_grad_one + jnp.einsum(
        "tq,dq->td", key_low_grad, attn_back[1], preferred_element_type=jnp.float32
    )
    norm_grad_one = norm_grad_one + jnp.einsum(
        "tq,dq->td", value_low_grad, attn_back[2], preferred_element_type=jnp.float32
    )
    weighted_one = gain_one * norm_grad_one
    gain_one_term = jnp.sum(norm_grad_one * inputs_f * scale_one, 0)
    tokens_grad = (
        residual_grad
        + scale_one * weighted_one
        - inputs_f * scale_one**3 * jnp.mean(weighted_one * inputs_f, -1, keepdims=True)
    )
    expert_local = lax.psum_scatter(
        expert_weight_term(expert_rows, pre_act, pair_grad, slot_grads).astype(jnp.bfloat16),
        "shard",
        scatter_dimension=0,
        tiled=True,
    )
    attn_share = (
        lax.psum_scatter(
            query_term.astype(jnp.bfloat16), "shard", scatter_dimension=0, tiled=True
        ).astype(jnp.float32),
        lax.psum_scatter(
            key_term.astype(jnp.bfloat16), "shard", scatter_dimension=0, tiled=True
        ).astype(jnp.float32),
        lax.psum_scatter(
            value_term.astype(jnp.bfloat16), "shard", scatter_dimension=0, tiled=True
        ).astype(jnp.float32),
        lax.psum_scatter(
            output_term.astype(jnp.bfloat16), "shard", scatter_dimension=0, tiled=True
        ).astype(jnp.float32),
        lax.psum_scatter(
            gain_one_term.astype(jnp.bfloat16), "shard", scatter_dimension=0, tiled=True
        ).astype(jnp.float32),
        lax.psum_scatter(
            gain_two_term.astype(jnp.bfloat16), "shard", scatter_dimension=0, tiled=True
        ).astype(jnp.float32),
        lax.psum_scatter(
            router_term.astype(jnp.bfloat16), "shard", scatter_dimension=0, tiled=True
        ).astype(jnp.float32),
    )
    totals = (
        lax.psum(attn_share[0].astype(jnp.bfloat16), "rep").astype(jnp.float32),
        lax.psum(attn_share[1].astype(jnp.bfloat16), "rep").astype(jnp.float32),
        lax.psum(attn_share[2].astype(jnp.bfloat16), "rep").astype(jnp.float32),
        lax.psum(attn_share[3].astype(jnp.bfloat16), "rep").astype(jnp.float32),
        lax.psum(attn_share[4].astype(jnp.bfloat16), "rep").astype(jnp.float32),
        lax.psum(attn_share[5].astype(jnp.bfloat16), "rep").astype(jnp.float32),
        lax.psum(attn_share[6].astype(jnp.bfloat16), "rep").astype(jnp.float32),
        lax.psum(expert_local, "rep").astype(jnp.float32),
    )
    expert_share = totals[7]
    summed = (totals[0], totals[1], totals[2], totals[3], totals[4], totals[5], totals[6])
    return (
        layer_out,
        tokens_grad,
        summed[0],
        summed[1],
        summed[2],
        summed[3],
        summed[4],
        summed[5],
        summed[6],
        expert_share[:, :2],
        expert_share[:, 2],
    )


def solution(mesh):
    return jax.shard_map(
        per_device,
        mesh=mesh,
        in_specs=(
            P(("shard", "rep"), None),
            P(("shard", "rep"), None),
            P(("shard", "rep"), None),
            P("shard", None),
            P("shard", None),
            P("shard", None),
            P("shard", None),
            P("shard"),
            P("shard"),
            P("shard", None),
            P("shard", None, None, None),
            P("shard", None, None),
        ),
        out_specs=(
            P(("shard", "rep"), None),
            P(("shard", "rep"), None),
            P("shard", None),
            P("shard", None),
            P("shard", None),
            P("shard", None),
            P("shard"),
            P("shard"),
            P("shard", None),
            P("shard", None, None, None),
            P("shard", None, None),
        ),
        check_vma=False,
    )
```

profile of v0, /device:TPU:0, one launch (start us, length us, event | category | flops | bytes accessed | tf_op | source)
XLA Modules:
  0.0 2173.3 jit_solution(5980615732889466810)
XLA Ops:
  11.2 5.2 all-gather
  16.5 4.3 all-gather.1
  25.2 15.5 scatter_custom_fusion
  40.8 15.1 gather_fusion.2
  55.9 4.4 all_gather.40
  64.0 3.1 convolution_convert_fusion.5
  67.1 24.1 %all-gather.13.cloned.1.call-done = bf16[1024,1024]{1,0:T(8,128)(2,1)} async-done(((bf16[512,1024]{1,0:T(8,128)(2,1)}), bf16[1024,1024]{1,0:T(8,128)(2,1)}) %all-gather.13.cloned.1.call-update) | async-done | bytes 2097168 | tf_op jit(solution)/shard_map/all_gather | solution.py:130
  91.2 3.0 fusion.64
  94.6 8.1 fusion.69
  102.7 8.3 fusion.7
  111.0 7.5 fusion.30
  118.6 7.1 all-gather.15.cloned.1.call-done
  125.7 3.0 multiply_reduce_fusion.2
  132.3 15.5 scatter_custom_fusion.1
  148.0 15.3 gather_fusion
  164.0 351.7 %all-gather.17.cloned.1.call-done = bf16[16,2,1024,512]{3,2,1,0:T(8,128)(2,1)} async-done(((bf16[8,2,1024,512]{3,2,1,0:T(8,128)(2,1)}), bf16[16,2,1024,512]{3,2,1,0:T(8,128)(2,1)}) %all-gather.17.cloned.1.call-update) | async-done | bytes 33554448 | tf_op jit(solution)/shard_map/all_gather | solution.py:181
  515.7 33.9 %convolution_bitcast_fusion = f32[2,16,288,512]{3,2,0,1:T(8,128)} fusion(bf16[16,288,1024,1]{2,1,3,0:T(8,128)(2,1)} %bitcast.204, bf16[16,2,1024,512]{3,2,1,0:T(8,128)(2,1)} %all-gather.17.cloned.1.call-done), kind=kOutput, calls=%fused_computation.44 | convolution fusion | flops 9663676416 | bytes 61865984 | tf_op jit(solution)/shard_map/ecd,etdf->tecf/dot_general | solution.py:81
  549.6 166.4 %all-gather.19.cloned.1.call-done = bf16[16,1024,512]{2,1,0:T(8,128)(2,1)} async-done(((bf16[8,1024,512]{2,1,0:T(8,128)(2,1)}), bf16[16,1024,512]{2,1,0:T(8,128)(2,1)}) %all-gather.19.cloned.1.call-update) | async-done | bytes 16777232 | tf_op jit(solution)/shard_map/all_gather | solution.py:182
  716.0 26.8 %fusion.19 = (bf16[1,16,288,512]{3,2,1,0:T(8,128)(2,1)}, bf16[1,16,288,512]{3,2,1,0:T(8,128)(2,1)}, bf16[16,288,512]{2,1,0:T(8,128)(2,1)}) fusion(f32[2,16,288,512]{3,2,0,1:T(8,128)} %convolution_bitcast_fusion, bf16[16,1024,512]{2,1,0:T(8,128)(2,1)} %all-gather.19.cloned.1.call-done, f32[16,288,1024]{2,1,0:T(8,128)} %bitcast.202, f32[16,288]{1,0:T(8,128)S(1)} %mul.543), kind=kOutput, calls=%fused_computation.52 | convolution fusion | flops 4876664832 | bytes 68700160 | tf_op jit(solution)/shard_map/ecd,edf->ecf/dot_general | solution.py:88
  742.8 23.2 %fusion = f32[16,288,1024,1]{2,1,0,3:T(8,128)} fusion(bf16[16,2,1024,512]{3,2,1,0:T(8,128)(2,1)} %all-gather.17.cloned.1.call-done, bf16[1,16,288,512]{3,2,1,0:T(8,128)(2,1)} %get-tuple-element.125, bf16[1,16,288,512]{3,2,1,0:T(8,128)(2,1)} %get-tuple-element.124), kind=kOutput, calls=%fused_computation.7 | convolution fusion | flops 9668395008 | bytes 61865984 | tf_op jit(solution)/shard_map/tecf,etdf->ecd/dot_general | solution.py:95
  766.0 28.7 %gather_fusion.3 = f32[4096,1024]{1,0:T(8,128)} fusion(f32[4608,1024]{1,0:T(8,128)} %bitcast.201, s32[4096]{0:T(1024)S(1)} %broadcast_clamp_fusion), kind=kCustom, calls=%fused_computation.3 | custom fusion | bytes 33570816 | tf_op jit(solution)/shard_map/gather | solution.py:220
  794.7 9.5 bitcast_reduce_fusion
  804.2 13.6 fusion.71
  817.8 28.8 %gather_fusion.1 = f32[4096,1024]{1,0:T(8,128)} fusion(f32[4608,1024]{1,0:T(8,128)} %bitcast.200, s32[4096]{0:T(1024)S(1)} %broadcast_clamp_fusion), kind=kCustom, calls=%fused_computation.1 | custom fusion | bytes 33570816 | tf_op jit(solution)/shard_map/gather | solution.py:185
  846.7 11.1 fusion.5
  858.0 3.3 multiply_reduce_fusion
  866.4 8.5 fusion.38
  874.9 11.4 fusion.2
  888.4 12.7 fusion.14
  901.1 2.6 fusion.37
  906.7 4.5 convolution_convert_fusion
  911.3 4.9 convolution_multiply_fusion
  917.6 2.8 convolution_convert_fusion.1
  920.4 18.8 convert_bitcast_fusion.1
  939.3 26.8 %convert_bitcast_fusion = bf16[16,2,1024,512]{2,3,1,0:T(8,128)(2,1)} fusion(bf16[16,288,1024,1]{2,1,3,0:T(8,128)(2,1)} %bitcast.205, bf16[1,16,288,512]{3,2,1,0:T(8,128)(2,1)} %get-tuple-element.125, bf16[1,16,288,512]{3,2,1,0:T(8,128)(2,1)} %get-tuple-element.124), kind=kOutput, calls=%fused_computation.9 | convolution fusion | flops 9685172224 | bytes 52428800 | tf_op jit(solution)/shard_map/ecd,tecf->etdf/dot_general | solution.py:103
  966.0 34.3 %pad_maximum_fusion = bf16[16,3,1024,512]{2,3,1,0:T(8,128)(2,1)} fusion(bf16[16,1,1024,512]{2,3,1,0:T(8,128)(2,1)} %convert_bitcast_fusion.1, bf16[16,2,1024,512]{2,3,1,0:T(8,128)(2,1)} %convert_bitcast_fusion), kind=kLoop, calls=%fused_computation.6 | loop fusion | flops 25165824 | bytes 100663296 | tf_op jit(solution)/shard_map/concatenate | solution.py:107
  1002.9 549.8 %reduce-scatter.17.cloned.1.call-done = bf16[8,3,1024,512]{2,3,1,0:T(8,128)(2,1)} async-done(((bf16[16,3,1024,512]{2,3,1,0:T(8,128)(2,1)}), bf16[8,3,1024,512]{2,3,1,0:T(8,128)(2,1)}) %reduce-scatter.17.cloned.1.call-update) | async-done | bytes 25165840 | tf_op jit(solution)/shard_map/reduce_scatter | solution.py:290
  1555.3 3.3 fusion.72
  1561.2 4.9 all-reduce.6
  1566.3 4.1 fusion.26
  1570.4 63.9 %all-reduce.4 = (bf16[512]{0:T(512)(128)(2,1)S(1)}, bf16[512]{0:T(512)(128)(2,1)S(1)}, bf16[512,16]{0,1:T(8,128)(2,1)S(1)}) all-reduce(bf16[512]{0:T(512)(128)(2,1)S(1)} %dynamic-slice.11, bf16[512]{0:T(512)(128)(2,1)S(1)} %dynamic-slice.13, ...), channel_id=1, replica_groups=mesh['shard'=2,'rep'=16] {'rep'}, use_global_device_ids=true, to_apply=%region_31.32 | all-reduce | flops 9216 | bytes 36864 | tf_op jit(solution)/shard_map/psum | solution.py:324
  1636.0 423.3 %all-reduce.9.cloned.1.call-done = (bf16[512,1024]{1,0:T(8,128)(2,1)}, bf16[512,512]{1,0:T(8,128)(2,1)}, bf16[512,512]{1,0:T(8,128)(2,1)}, bf16[512,1024]{1,0:T(8,128)(2,1)}, bf16[8,3,1024,512]{2,3,1,0:T(8,128)(2,1)}) async-done(((bf16[512,1024]{1,0:T(8,128)(2,1)}, bf16[512,512]{1,0:T(8,128)(2,1)}, bf16[512,512]{1,0:T(8,128)(2,1)}, bf16[512,1024]{1,0:T(8,128)(2,1)}, bf16[8,3,1024,512]{2,3,1,0:T(8,128)(2,1)}), ...) | async-done | bytes 28311568 | tf_op jit(solution)/shard_map/psum | solution.py:320
  2059.4 19.1 slice.129
  2078.5 6.0 copy-done
  2084.4 16.4 convert_element_type.200
  2106.2 31.9 %copy.117 = f32[8,2,1024,512]{3,2,1,0:T(8,128)} copy(f32[8,2,1024,512]{2,3,1,0:T(8,128)} %slice.129) | data formatting | bytes 67108864
  2138.1 11.8 slice_bitcast_fusion
  2149.9 16.4 copy.118
  (235 shorter events, 42.3 us)
Async XLA Ops:
  7.2 54.5 %all-gather.11.cloned.1.call-start = ((), (), s32[]{:S(2)}) async-start(), calls=%async_computation.7 | async-start | bytes 1572864 | tf_op jit(solution)/shard_map/all_gather | solution.py:131
  7.9 56.0 %all-gather.9.cloned.1.call-start = ((), (), s32[]{:S(2)}) async-start(), calls=%async_computation.6 | async-start | bytes 1572864 | tf_op jit(solution)/shard_map/all_gather | solution.py:132
  8.7 82.5 %all-gather.13.cloned.1.call-start = ((), (), s32[]{:S(2)}) async-start(), calls=%async_computation.8 | async-start | bytes 3145728 | tf_op jit(solution)/shard_map/all_gather | solution.py:130
  9.4 116.3 %all-gather.15.cloned.1.call-start = ((), (), s32[]{:S(2)}) async-start(), calls=%async_computation.9 | async-start | bytes 3145728 | tf_op jit(solution)/shard_map/all_gather | solution.py:133
  10.0 505.8 %all-gather.17.cloned.1.call-start = ((), (), s32[]{:S(2)}) async-start(), calls=%async_computation.10 | async-start | bytes 50331648 | tf_op jit(solution)/shard_map/all_gather | solution.py:181
  10.6 10.3 copy-start.41
  10.6 12.7 copy-start.11
  10.6 705.4 %all-gather.19.cloned.1.call-start = ((), (), s32[]{:S(2)}) async-start(), calls=%async_computation.11 | async-start | bytes 25165824 | tf_op jit(solution)/shard_map/all_gather | solution.py:182
  11.2 991.6 %reduce-scatter.11.cloned.1.call-start = ((), (), s32[]{:S(2)}) async-start(), calls=%async_computation.14 | async-start | bytes 1572864 | tf_op jit(solution)/shard_map/reduce_scatter | solution.py:303
  16.5 74.7 %copy-start.51 = (f32[2,1,512]{2,1,0:T(1,128)}, f32[2,1,512]{2,1,0:T(1,128)S(1)}, u32[]{:S(2)}) copy-start(f32[2,1,512]{2,1,0:T(1,128)S(1)} %convert_element_type.201) | copy-start | bytes 12292
  20.9 108.5 %copy-start.47 = (f32[2,1,512]{2,1,0:T(1,128)}, f32[2,1,512]{2,1,0:T(1,128)S(1)}, u32[]{:S(2)}) copy-start(f32[2,1,512]{2,1,0:T(1,128)S(1)} %convert_element_type.202) | copy-start | bytes 12292
  40.7 15.1 copy-start.59
  40.8 19.6 copy-start.7
  60.3 70.1 %copy-start.43 = (bf16[1024,16]{0,1:T(8,128)(2,1)}, bf16[1024,16]{0,1:T(8,128)(2,1)S(1)}, u32[]{:S(2)}) copy-start(bf16[1024,16]{0,1:T(8,128)(2,1)S(1)} %all_gather.40) | copy-start | bytes 98308
  61.3 29.9 %copy-start.57 = (f32[512]{0:T(512)}, f32[512]{0:T(512)S(1)}, u32[]{:S(2)}) copy-start(f32[512]{0:T(512)S(1)} %get-tuple-element.138) | copy-start | bytes 6148
  61.6 32.6 %copy-start.20 = (f32[512,32]{0,1:T(8,128)}, f32[512,32]{0,1:T(8,128)S(1)}, u32[]{:S(2)}) copy-start(f32[512,32]{0,1:T(8,128)S(1)} %get-tuple-element.141) | copy-start | bytes 196612
  61.6 32.6 %copy-start.22 = (f32[512,32]{0,1:T(8,128)}, f32[512,32]{0,1:T(8,128)S(1)}, u32[]{:S(2)}) copy-start(f32[512,32]{0,1:T(8,128)S(1)} %get-tuple-element.142) | copy-start | bytes 196612
  63.9 30.7 %copy-start.28 = (bf16[512,8,32]{0,2,1:T(8,128)(2,1)}, bf16[512,8,32]{0,2,1:T(8,128)(2,1)S(1)}, u32[]{:S(2)}) copy-start(bf16[512,8,32]{0,2,1:T(8,128)(2,1)S(1)} %get-tuple-element.135) | copy-start | bytes 786436
  63.9 30.7 %copy-start.30 = (bf16[512,8,32]{0,2,1:T(8,128)(2,1)}, bf16[512,8,32]{0,2,1:T(8,128)(2,1)S(1)}, u32[]{:S(2)}) copy-start(bf16[512,8,32]{0,2,1:T(8,128)(2,1)S(1)} %get-tuple-element.136) | copy-start | bytes 786436
  102.7 8.3 copy-start.36
  118.6 10.8 copy-start.32
  130.3 33.0 %copy-start.5 = (bf16[512,1024]{1,0:T(8,128)(2,1)}, bf16[512,1024]{1,0:T(8,128)(2,1)S(1)}, u32[]{:S(2)}) copy-start(bf16[512,1024]{1,0:T(8,128)(2,1)S(1)} %multiply_convert_fusion.7) | copy-start | bytes 3145732
  132.2 15.7 copy-start.13
  148.0 568.1 %copy-start.45 = (f32[16,288]{1,0:T(8,128)}, f32[16,288]{1,0:T(8,128)S(1)}, u32[]{:S(2)}) copy-start(f32[16,288]{1,0:T(8,128)S(1)} %mul.543) | copy-start | bytes 55300
  817.8 28.8 %copy-start.14 = (f32[512,8]{1,0:T(8,128)S(1)}, f32[512,8]{1,0:T(8,128)}, u32[]{:S(2)}) copy-start(f32[512,8]{1,0:T(8,128)} %copy-done.13) | copy-start | bytes 49156
  846.6 11.3 copy-start.35
  846.6 11.3 copy-start.50
  846.6 11.3 copy-start.54
  846.6 11.3 copy-start.42
  846.6 11.4 copy-start.3
  846.6 11.4 copy-start.44
  846.6 11.4 copy-start.48
  846.6 11.4 copy-start.56
  866.3 8.5 copy-start.37
  874.9 11.5 copy-start.8
  874.9 11.5 copy-start.52
  874.9 11.5 copy-start.58
  888.3 114.5 %reduce-scatter.9.cloned.1.call-start = ((), (), s32[]{:S(2)}) async-start(), calls=%async_computation.13 | async-start | bytes 1572864 | tf_op jit(solution)/shard_map/reduce_scatter | solution.py:300
  888.3 12.7 copy-start.16
  888.3 12.7 copy-start.18
  906.6 96.2 %reduce-scatter.13.cloned.1.call-start = ((), (), s32[]{:S(2)}) async-start(), calls=%async_computation.15 | async-start | bytes 3145728 | tf_op jit(solution)/shard_map/reduce_scatter | solution.py:306
  911.2 91.7 %reduce-scatter.7.cloned.1.call-start = ((), (), s32[]{:S(2)}) async-start(), calls=%async_computation.12 | async-start | bytes 3145728 | tf_op jit(solution)/shard_map/reduce_scatter | solution.py:297
  939.2 613.4 %reduce-scatter.17.cloned.1.call-start = ((), (), s32[]{:S(2)}) async-start(), calls=%async_computation.17 | async-start | bytes 75497472 | tf_op jit(solution)/shard_map/reduce_scatter | solution.py:290
  1000.3 570.0 %reduce-scatter.15.cloned.1.call-start = ((), (), s32[]{:S(2)}) async-start(), calls=%async_computation.16 | async-start | bytes 49152 | tf_op jit(solution)/shard_map/reduce_scatter | solution.py:315
  1002.7 1056.7 %all-reduce.9.cloned.1.call-start = ((), (), s32[]{:S(2)}) async-start(), calls=%async_computation.18 | async-start | bytes 56623104 | tf_op jit(solution)/shard_map/psum | solution.py:320
  2059.4 25.1 %copy-start = (bf16[8,3,1024,512]{2,3,1,0:T(8,128)(2,1)S(1)}, bf16[8,3,1024,512]{2,3,1,0:T(8,128)(2,1)}, u32[]{:S(2)}) copy-start(bf16[8,3,1024,512]{2,3,1,0:T(8,128)(2,1)} %get-tuple-element.119) | copy-start | bytes 75497472
  2084.4 16.4 copy-start.26
  2084.4 18.0 copy-start.39
  (30 other events, 91.8 us)
Sparse Core Ops, SparseCore 0:
  9.6 23.9 all-gather.10
  35.1 21.3 all-gather.8
  58.0 33.1 all-gather.12
  92.6 33.1 all-gather.14
  127.1 388.5 all-gather.16
  517.1 198.8 all-gather.18
  888.4 20.3 reduce-scatter.10
  911.7 20.3 reduce-scatter.8
  934.9 31.8 reduce-scatter.12
  969.5 31.8 reduce-scatter.6
  1003.7 548.9 reduce-scatter.16
  1555.3 9.8 reduce-scatter.14
  1570.3 489.0 all-reduce.8
where the time goes:
time: 2180 us; the launch traced here: 2170 us
  waiting for transfers between devices  1530 us (70%)
  matrix products  221 us (10%)
  local copies, waits for them, and re-layouts  215 us (10%)
  other arithmetic  111 us (5%)
  blocking collectives  82.8 us (4%)
    reduce_scatter x1, waiting for transfers between devices, per_device(): lax.psum_scatter(expert_weight_term(expert_rows, pre_act, pair_grad, slot...  550 us
    psum x1, waiting for transfers between devices, per_device(): lax.psum(attn_share[0].astype(jnp.bfloat16), 'rep').astype(jnp.float32)  423 us
    all_gather x1, waiting for transfers between devices, per_device(): lax.all_gather(expert_in, 'shard', axis=0, tiled=True)  352 us
    all_gather x1, waiting for transfers between devices, per_device(): lax.all_gather(expert_out, 'shard', axis=0, tiled=True)  166 us
    psum x1, blocking collectives, per_device(): lax.psum(attn_share[4].astype(jnp.bfloat16), 'rep').astype(jnp.float32)  63.9 us
    unnamed x137, local copies, waits for them, and re-layouts  63.2 us
  transfers between devices with their start and end apart: 13, of which 6 were waited for; matrix products, arithmetic and copies ran while one was open for 12% of the time, Pallas kernels for 0%

commit v1 on v0

v1 whole, which is shorter than its diff:
```python
import functools

import jax
import jax.numpy as jnp
from jax import lax
from jax.sharding import PartitionSpec as P

D = 1024
HEADS = 16
KV_HEADS = 8
HEAD_DIM = 64
EXPERTS = 16
SEQ = 512
CAP = 288


EPSILON = 1e-06
ATTN_SCALE = 0.015625
RESIDUAL_SCALE = 0.22
ROPE_BASE = 10000.0


def rope_tables(length, width):
    half_width = width // 2
    frequency = ROPE_BASE ** (-2.0 * jnp.arange(half_width, dtype=jnp.float32) / width)
    angles = jnp.arange(length, dtype=jnp.float32)[:, None] * frequency[None, :]
    return (jnp.cos(angles)[:, None, :], jnp.sin(angles)[:, None, :])


def rotate(values, cosine, sine_part):
    half_width = values.shape[-1] // 2
    first_half = values[..., :half_width]
    second_half = values[..., half_width:]
    return jnp.concatenate(
        [
            first_half * cosine - second_half * sine_part,
            second_half * cosine + first_half * sine_part,
        ],
        -1,
    )


def unrotate(values, cosine, sine_part):
    half_width = values.shape[-1] // 2
    first_half = values[..., :half_width]
    second_half = values[..., half_width:]
    return jnp.concatenate(
        [
            first_half * cosine + second_half * sine_part,
            second_half * cosine - first_half * sine_part,
        ],
        -1,
    )


def block_scores(query_block, key_block, first_row):
    scores = ATTN_SCALE * jnp.einsum(
        "sqgjd,skgd->sgjqk", query_block, key_block, preferred_element_type=jnp.float32
    )
    query_pos = first_row + jnp.arange(query_block.shape[1])
    key_pos = jnp.arange(key_block.shape[1])
    return jnp.where(query_pos[:, None] >= key_pos[None, :], scores, -jnp.inf)


def shift(value, axis, size, step):
    return lax.ppermute(value, axis, [(i, (i + step) % size) for i in range(size)])


def after(value, *others):
    return lax.optimization_barrier((value,) + others)[0]


def gather_rows(block, shards, reps):
    me = lax.axis_index("shard")
    odd = lax.rem(lax.axis_index("rep"), 2)
    rows, width = block.shape
    half = rows // 2
    mine = lax.dynamic_slice_in_dim(block, odd * half, half, 0)
    swap = [(i, i ^ 1) for i in range(reps)]
    whole = jnp.zeros((shards * rows, width), block.dtype)
    whole = lax.dynamic_update_slice_in_dim(whole, block, me * rows, 0)
    for step in range(1, shards):
        owner = lax.rem(me - step + shards, shards)
        first = shift(mine, "shard", shards, step)
        second = lax.ppermute(first, "rep", swap)
        whole = lax.dynamic_update_slice_in_dim(whole, first, owner * rows + odd * half, 0)
        whole = lax.dynamic_update_slice_in_dim(whole, second, owner * rows + (1 - odd) * half, 0)
    return whole


def per_device(
    shards,
    reps,
    tokens,
    routes,
    out_grad,
    query_weight,
    key_weight,
    value_weight,
    output_weight,
    norm_one,
    norm_two,
    router_weight,
    expert_in,
    expert_out,
):
    row_count = tokens.shape[0]
    seq_count = row_count // SEQ
    group_heads = HEADS // KV_HEADS
    query_width = HEADS * HEAD_DIM
    kv_width = KV_HEADS * HEAD_DIM
    local = EXPERTS // shards
    low = jnp.bfloat16
    me = lax.axis_index("shard")
    side = jnp.concatenate(
        [router_weight, norm_one[:, None], norm_two[:, None]]
        + [jnp.zeros((router_weight.shape[0], 128 - EXPERTS - 2), low)],
        1,
    )
    first_full = gather_rows(
        jnp.concatenate([query_weight, key_weight, value_weight, side], 1), shards, reps
    )
    output_full = gather_rows(after(output_weight, first_full), shards, reps)
    qkv_full = first_full[:, : query_width + 2 * kv_width]
    query_full = first_full[:, :query_width]
    key_full = first_full[:, query_width : query_width + kv_width]
    value_full = first_full[:, query_width + kv_width : query_width + 2 * kv_width]
    base = query_width + 2 * kv_width
    router_full = first_full[:, base : base + EXPERTS]
    gain_one = first_full[:, base + EXPERTS].astype(jnp.float32)
    gain_two = first_full[:, base + EXPERTS + 1].astype(jnp.float32)
    grad_send = after(out_grad, output_full)
    grad_groups = [out_grad] + [shift(grad_send, "shard", shards, k) for k in range(1, shards)]
    route_groups = [routes] + [shift(routes, "shard", shards, k) for k in range(1, shards)]

    inputs_f = tokens.astype(jnp.float32)
    scale_one = lax.rsqrt(jnp.mean(inputs_f * inputs_f, -1, keepdims=True) + EPSILON)
    normed_one = (inputs_f * scale_one * gain_one).astype(low)
    query_pre = jnp.dot(normed_one, query_full, preferred_element_type=jnp.float32)
    key_pre = jnp.dot(normed_one, key_full, preferred_element_type=jnp.float32)
    value_low = jnp.dot(normed_one, value_full, preferred_element_type=jnp.float32).astype(low)
    value_low = value_low.reshape(seq_count, SEQ, KV_HEADS, HEAD_DIM)
    cosine, sine_part = rope_tables(SEQ, HEAD_DIM)
    queries = rotate(query_pre.reshape(seq_count, SEQ, HEADS, HEAD_DIM), cosine, sine_part).astype(
        low
    )
    queries = queries.reshape(seq_count, SEQ, KV_HEADS, group_heads, HEAD_DIM)
    keys_low = rotate(
        key_pre.reshape(seq_count, SEQ, KV_HEADS, HEAD_DIM), cosine, sine_part
    ).astype(low)
    scores = block_scores(queries, keys_low, 0)
    row_max = jnp.max(scores, -1, keepdims=True)
    exp_scores = jnp.exp(scores - row_max)
    row_total = jnp.sum(exp_scores, -1, keepdims=True)
    prob_low = (exp_scores / row_total).astype(low)
    head_outputs = jnp.einsum(
        "sgjqk,skgd->sqgjd", prob_low, value_low, preferred_element_type=jnp.float32
    )
    log_total = row_max + jnp.log(row_total)
    attended = head_outputs.reshape(row_count, query_width).astype(low)
    branch = jnp.dot(attended, output_full, preferred_element_type=jnp.float32)
    residual = inputs_f + RESIDUAL_SCALE * branch
    scale_two = lax.rsqrt(jnp.mean(residual * residual, -1, keepdims=True) + EPSILON)
    normed_two = (residual * scale_two * gain_two).astype(low)

    group_rows = [normed_two] + [shift(normed_two, "shard", shards, k) for k in range(1, shards)]
    experts_iota = jnp.arange(EXPERTS, dtype=jnp.int32)
    triangle = (jnp.arange(row_count)[:, None] > jnp.arange(row_count)[None, :]).astype(low)

    def gates_of(rows, group_routes):
        named = jnp.any(group_routes[:, :, None] == experts_iota, 1)
        logits = jnp.dot(rows, router_full, preferred_element_type=jnp.float32)
        return named, jax.nn.softmax(jnp.where(named, logits, -jnp.inf), -1)

    def mine_of(table):
        return lax.dynamic_slice_in_dim(table, me * local, local, 1)

    spreads, rows_slots, grad_slots, gate_slots = [], [], [], []
    slots = jnp.arange(CAP, dtype=jnp.int32)
    home = None
    for k in range(shards):
        named, gates = gates_of(group_rows[k], route_groups[k])
        if k == 0:
            home = (named, gates)
        ranks = jnp.dot(triangle, named.astype(low), preferred_element_type=jnp.float32)
        ranks = jnp.where(named, ranks.astype(jnp.int32), -1)
        place = mine_of(ranks).T
        hit = place[:, None, :] == slots[None, :, None]
        spread = hit.astype(low)
        spreads.append(spread)
        flat = spread.reshape(local * CAP, row_count)
        rows_slots.append(
            jnp.dot(flat, group_rows[k], preferred_element_type=jnp.float32)
            .astype(low)
            .reshape(local, CAP, D)
        )
        grad_slots.append(
            jnp.dot(flat, grad_groups[k], preferred_element_type=jnp.float32)
            .astype(low)
            .reshape(local, CAP, D)
        )
        gate_slots.append(jnp.sum(jnp.where(hit, mine_of(gates).T[:, None, :], 0.0), -1))
    rows_in = jnp.concatenate(rows_slots, 1)
    grads_in = jnp.concatenate(grad_slots, 1)
    slot_gate = jnp.concatenate(gate_slots, 1)[:, :, None] * RESIDUAL_SCALE

    def up(part):
        return jnp.einsum(
            "ecd,edf->ecf", rows_in, expert_in[:, part], preferred_element_type=jnp.float32
        )

    gate_act, up_act = up(0), up(1)
    sigmoid = jax.nn.sigmoid(gate_act)
    hidden = gate_act * sigmoid * up_act
    scaled_hidden = (slot_gate * hidden).astype(low)
    out_term = jnp.einsum(
        "ecd,ecf->edf", grads_in, scaled_hidden, preferred_element_type=jnp.float32
    ).astype(low)
    out_total = lax.psum(out_term, "rep")
    hidden_grad = jnp.einsum(
        "ecd,edf->ecf", grads_in, expert_out, preferred_element_type=jnp.float32
    )
    gate_grad_slots = RESIDUAL_SCALE * jnp.sum(hidden * hidden_grad, -1)
    hidden_grad = slot_gate * hidden_grad
    gate_side = (hidden_grad * up_act * sigmoid * (1.0 + gate_act * (1.0 - sigmoid))).astype(low)
    up_side = (hidden_grad * (gate_act * sigmoid)).astype(low)
    pair_side = jnp.stack([gate_side, up_side])
    rows_grad = jnp.einsum(
        "tecf,etdf->ecd", pair_side, expert_in, preferred_element_type=jnp.float32
    ).astype(low)
    mixed = jnp.einsum(
        "ecf,edf->ecd", scaled_hidden, expert_out, preferred_element_type=jnp.float32
    ).astype(low)

    norm_grad_two, gate_grad_parts, mix = None, [], None
    for k in range(shards):
        span = slice(k * CAP, (k + 1) * CAP)
        spread = spreads[k].reshape(local * CAP, row_count)

        def collect(values):
            return jnp.einsum(
                "st,sd->td",
                spread,
                values[:, span].reshape(local * CAP, D),
                preferred_element_type=jnp.float32,
            )

        rows_part = collect(rows_grad)
        mix_part = collect(mixed)
        gate_part = jnp.sum(
            jnp.where(spreads[k] > 0, gate_grad_slots[:, span][:, :, None], 0.0), 1
        )
        if k == 0:
            norm_grad_two, mix = rows_part, mix_part
        else:
            norm_grad_two = norm_grad_two + shift(rows_part.astype(low), "shard", shards, -k)
            mix = mix + shift(mix_part.astype(low), "shard", shards, -k)
            gate_part = shift(gate_part, "shard", shards, -k)
        gate_grad_parts.append(gate_part)
    layer_out = (residual + mix).astype(low)

    in_terms = [
        jnp.einsum("ecd,ecf->edf", rows_in, part, preferred_element_type=jnp.float32).astype(low)
        for part in (gate_side, up_side)
    ]
    gate_total = lax.psum(after(in_terms[0], out_total), "rep")
    up_total = lax.psum(after(in_terms[1], gate_total), "rep")

    gate_grad = jnp.zeros((EXPERTS, row_count), jnp.float32)
    for k in range(shards):
        start = lax.rem(me + k, shards) * local
        gate_grad = lax.dynamic_update_slice_in_dim(gate_grad, gate_grad_parts[k], start, 0)
    gate_grad = gate_grad.T
    gates = home[1]
    logit_grad = gates * (gate_grad - jnp.sum(gates * gate_grad, -1, keepdims=True))
    grad_out = out_grad.astype(jnp.float32)
    exact = lax.Precision.HIGHEST
    norm_grad_two = norm_grad_two + jnp.dot(
        logit_grad, router_full.astype(jnp.float32).T, precision=exact
    )
    router_term = jnp.dot(normed_two.astype(jnp.float32).T, logit_grad, precision=exact)
    weighted_two = gain_two * norm_grad_two
    gain_two_term = jnp.sum(norm_grad_two * residual * scale_two, 0)
    residual_grad = (
        grad_out
        + scale_two * weighted_two
        - residual * scale_two**3 * jnp.mean(weighted_two * residual, -1, keepdims=True)
    )
    branch_grad = (RESIDUAL_SCALE * residual_grad).astype(low)
    output_term = jnp.einsum("tq,td->qd", attended, branch_grad, preferred_element_type=jnp.float32)
    attended_grad = jnp.einsum(
        "td,qd->tq", branch_grad, output_full, preferred_element_type=jnp.float32
    ).astype(low)
    attended_grad = attended_grad.reshape(seq_count, SEQ, KV_HEADS, group_heads, HEAD_DIM)
    scores = block_scores(queries, keys_low, 0)
    probs_f = jnp.exp(scores - log_total)
    prob_low = probs_f.astype(low)
    value_grad = jnp.einsum(
        "sgjqk,sqgjd->skgd", prob_low, attended_grad, preferred_element_type=jnp.float32
    )
    prob_grad = jnp.einsum(
        "sqgjd,skgd->sgjqk", attended_grad, value_low, preferred_element_type=jnp.float32
    )
    score_grad = (
        probs_f * (prob_grad - jnp.sum(probs_f * prob_grad, -1, keepdims=True))
    ).astype(low)
    query_grad = ATTN_SCALE * jnp.einsum(
        "sgjqk,skgd->sqgjd", score_grad, keys_low, preferred_element_type=jnp.float32
    )
    key_grad = ATTN_SCALE * jnp.einsum(
        "sgjqk,sqgjd->skgd", score_grad, queries, preferred_element_type=jnp.float32
    )
    query_low = unrotate(query_grad.reshape(seq_count, SEQ, HEADS, HEAD_DIM), cosine, sine_part)
    key_low = unrotate(key_grad, cosine, sine_part)
    qkv_low = jnp.concatenate(
        [
            query_low.reshape(row_count, query_width).astype(low),
            key_low.reshape(row_count, kv_width).astype(low),
            value_grad.reshape(row_count, kv_width).astype(low),
        ],
        1,
    )
    qkv_term = jnp.einsum("td,tq->dq", normed_one, qkv_low, preferred_element_type=jnp.float32)
    norm_grad_one = jnp.einsum(
        "tq,dq->td", qkv_low, qkv_full, preferred_element_type=jnp.float32
    )
    weighted_one = gain_one * norm_grad_one
    gain_one_term = jnp.sum(norm_grad_one * inputs_f * scale_one, 0)
    tokens_grad = (
        residual_grad
        + scale_one * weighted_one
        - inputs_f * scale_one**3 * jnp.mean(weighted_one * inputs_f, -1, keepdims=True)
    )
    small = jnp.concatenate(
        [
            qkv_term.astype(low),
            output_term.astype(low),
            router_term.astype(low),
            gain_one_term[:, None].astype(low),
            gain_two_term[:, None].astype(low),
            jnp.zeros((D, 128 - EXPERTS - 2), low),
        ],
        1,
    )
    own = D // shards

    def rows_for(step):
        return lax.dynamic_slice_in_dim(small, lax.rem(me + step, shards) * own, own, 0)

    share = rows_for(0).astype(jnp.float32)
    for k in range(1, shards):
        share = share + shift(rows_for(k), "shard", shards, k)
    share = after(share.astype(low), up_total)
    total = lax.psum(share, "rep").astype(jnp.float32)
    base = query_width + 2 * kv_width
    side = total[:, base + D :]
    return (
        layer_out,
        tokens_grad,
        total[:, :query_width],
        total[:, query_width : query_width + kv_width],
        total[:, query_width + kv_width : base],
        total[:, base : base + D],
        side[:, EXPERTS],
        side[:, EXPERTS + 1],
        side[:, :EXPERTS],
        jnp.stack([gate_total, up_total], 1).astype(jnp.float32),
        out_total.astype(jnp.float32),
    )


def solution(mesh):
    return jax.shard_map(
        functools.partial(per_device, mesh.shape["shard"], mesh.shape["rep"]),
        mesh=mesh,
        in_specs=(
            P(("shard", "rep"), None),
            P(("shard", "rep"), None),
            P(("shard", "rep"), None),
            P("shard", None),
            P("shard", None),
            P("shard", None),
            P("shard", None),
            P("shard"),
            P("shard"),
            P("shard", None),
            P("shard", None, None, None),
            P("shard", None, None),
        ),
        out_specs=(
            P(("shard", "rep"), None),
            P(("shard", "rep"), None),
            P("shard", None),
            P("shard", None),
            P("shard", None),
            P("shard", None),
            P("shard"),
            P("shard"),
            P("shard", None),
            P("shard", None, None, None),
            P("shard", None, None),
        ),
        check_vma=False,
    )
```

time: 2180 us -> 906 us (0.42)
  waiting for transfers between devices: 1530 us -> 496 us
  local copies, waits for them, and re-layouts: 215 us -> 61.1 us
  blocking collectives: 82.8 us -> 0 us
  other arithmetic: 111 us -> 82.8 us
    reduce_scatter x6 -> x0, waiting for transfers between devices: 550 us -> none  [the longest x1 550 us: per_device(): lax.psum_scatter(expert_weight_term(expert_rows, pre_act, pair_grad, slot...]
    all_gather x6 -> x0, waiting for transfers between devices: 549 us -> none  [the longest x1 352 us: per_device(): lax.all_gather(expert_in, 'shard', axis=0, tiled=True)]
    gather x4 -> x0, local copies, waits for them, and re-layouts: 87.9 us -> none  [the longest x1 28.8 us: per_device(): slot_values = result.reshape(EXPERTS * CAP, D)[slot_of]]
    psum x1 -> x0, blocking collectives: 63.9 us -> none  [per_device(): lax.psum(attn_share[4].astype(jnp.bfloat16), 'rep').astype(jnp.float32)]
    ppermute x0 -> x11, waiting for transfers between devices: none -> 59.2 us  [the longest x9 59.2 us: shift(): lax.ppermute(value, axis, [(i, (i + step) % size) for i in range(size)])]
    unnamed x137 -> x129, local copies, waits for them, and re-layouts: 63.2 us -> 21.8 us
    concatenate x1 -> x0, other arithmetic: 34.3 us -> none  [expert_weight_term(): return jnp.concatenate([in_term, out_term[:, None]], 1)]
    scatter x2 -> x0, local copies, waits for them, and re-layouts: 31.1 us -> none  [the longest x1 15.5 us: dispatch(): token_of = jnp.full((EXPERTS * CAP,), token_count, jnp.int32).at[slot_of....]
  transfers between devices with their start and end apart: 13 -> 15, of which waited for: 6 -> 8; matrix products, arithmetic and copies ran while one was open for 12% -> 35% of each run, Pallas kernels for 0% -> 0%
where the time goes in v1:
time: 906 us; the launch traced here: 898 us
  waiting for transfers between devices  496 us (55%)
  matrix products  229 us (25%)
  other arithmetic  82.8 us (9%)
  local copies, waits for them, and re-layouts  61.1 us (7%)
  between operations  15 us (2%)
  starting transfers between devices  13 us (1%)
    psum x1, waiting for transfers between devices, per_device(): gate_total = lax.psum(after(in_terms[0], out_total), 'rep')  128 us
    psum x1, waiting for transfers between devices, per_device(): out_total = lax.psum(out_term, 'rep')  113 us
    psum x1, waiting for transfers between devices, per_device(): up_total = lax.psum(after(in_terms[1], gate_total), 'rep')  107 us
    psum x1, waiting for transfers between devices, per_device(): total = lax.psum(share, 'rep').astype(jnp.float32)  88.6 us
    ppermute x9, waiting for transfers between devices, shift(): lax.ppermute(value, axis, [(i, (i + step) % size) for i in range(size)])  59.2 us
    dot_general x4, matrix products, collect(): jnp.einsum('st,sd->td', spread, values[:, span].reshape(local * CAP, D),...  24.7 us
    dot_general x2, matrix products, per_device(): jnp.einsum('ecd,ecf->edf', rows_in, part, preferred_element_type=jnp.floa...  24.6 us
    unnamed x129, local copies, waits for them, and re-layouts  21.8 us
  transfers between devices with their start and end apart: 15, of which 8 were waited for; matrix products, arithmetic and copies ran while one was open for 35% of the time, Pallas kernels for 0%

profile of v1, /device:TPU:0, one launch (start us, length us, event | category | flops | bytes accessed | tf_op | source)
XLA Modules:
  0.0 897.5 jit_solution(4233610000031689438)
XLA Ops:
  11.1 3.8 concatenate.55
  16.0 2.9 collective-permute-start
  27.3 16.7 %collective-permute-done.4 = s32[512,8]{0,1:T(8,128)S(1)} collective-permute-done((s32[512,8]{0,1:T(8,128)S(1)}, s32[512,8]{0,1:T(8,128)S(1)}, u32[]{:S(2)}, u32[]{:S(2)}) %collective-permute-start.4) | collective-permute-done | bytes 16416 | tf_op jit(solution)/shard_map/ppermute | solution.py:66
  47.9 5.5 convolution_convert_fusion.5
  58.8 3.0 fusion.46
  66.4 8.1 fusion.112
  74.5 8.2 fusion.3
  85.1 7.5 fusion.57
  100.2 2.8 convolution_convert_fusion.7
  103.1 19.8 %collective-permute-done.5 = bf16[512,1024]{1,0:T(8,128)(2,1)S(1)} collective-permute-done((bf16[512,1024]{1,0:T(8,128)(2,1)S(1)}, bf16[512,1024]{1,0:T(8,128)(2,1)S(1)}, u32[]{:S(2)}, u32[]{:S(2)}) %collective-permute-start.5) | collective-permute-done | bytes 1048608 | tf_op jit(solution)/shard_map/ppermute | solution.py:66
  122.9 4.2 convolution_convert_fusion.6
  127.1 10.4 %fusion.15 = f32[8,576,512]{2,1,0:T(8,128)} fusion(bf16[8,288,1024]{2,1,0:T(8,128)(2,1)} %bitcast.224, bf16[8,288,1024]{2,1,0:T(8,128)(2,1)S(1)} %bitcast.220, bf16[8,2,1024,512]{3,2,1,0:T(8,128)(2,1)} %param.22), kind=kOutput, calls=%fused_computation.31 | convolution fusion | flops 4850712576 | bytes 27262976 | tf_op jit(solution)/shard_map/ecd,edf->ecf/dot_general | solution.py:208
  137.4 10.5 %fusion.14 = f32[8,576,512]{2,1,0:T(8,128)} fusion(bf16[8,288,1024]{2,1,0:T(8,128)(2,1)} %bitcast.225, bf16[8,288,1024]{2,1,0:T(8,128)(2,1)S(1)} %bitcast.221, bf16[8,2,1024,512]{3,2,1,0:T(8,128)(2,1)} %param.22), kind=kOutput, calls=%fused_computation.29 | convolution fusion | flops 4850712576 | bytes 27262976 | tf_op jit(solution)/shard_map/ecd,edf->ecf/dot_general | solution.py:208
  148.0 4.2 convolution_convert_fusion.4
  152.2 18.4 %multiply_reduce_fusion = (f32[8,576]{1,0:T(8,128)S(1)}, f32[8,576,512]{2,1,0:T(8,128)}) fusion(f32[8,576,512]{2,1,0:T(8,128)} %fusion.14, f32[8,576,512]{2,1,0:T(8,128)} %fusion.15, bf16[8,1024,512]{2,1,0:T(8,128)(2,1)} %param.23, bf16[8,288,1024]{2,1,0:T(8,128)(2,1)} %bitcast.218, bf16[8,288,1024]{2,1,0:T(8,128)(2,1)} %bitcast.216), kind=kOutput, calls=%fused_computation.19 | convolution fusion | flops 4867223040 | bytes 46155776 | tf_op jit(solution)/shard_map/ecd,edf->ecf/dot_general | solution.py:220
  176.4 15.1 %multiply_convert_fusion.1 = (bf16[8,576,512]{2,1,0:T(8,128)(2,1)}, bf16[8,576,512]{2,1,0:T(8,128)(2,1)S(1)}, bf16[8,576,512]{2,1,0:T(8,128)(2,1)}) fusion(f32[8,576,512]{2,1,0:T(8,128)} %fusion.15, f32[8,576,512]{2,1,0:T(8,128)} %fusion.14, f32[8,576,512]{2,1,0:T(8,128)} %get-tuple-element.109, f32[8,576]{1,0:T(8,128)S(1)} %maximum_multiply_fusion), kind=kLoop, calls=%fused_computation.21 | loop fusion | flops 40108032 | bytes 42485760 | tf_op jit(solution)/shard_map/convert_element_type | solution.py:225
  193.7 11.8 %convolution_convert_fusion.2 = bf16[8,1024,512]{2,1,0:T(8,128)(2,1)} fusion(bf16[8,576,512]{2,1,0:T(8,128)(2,1)S(1)} %get-tuple-element.78, bf16[8,288,1024]{2,1,0:T(8,128)(2,1)} %bitcast.226, bf16[8,288,1024]{2,1,0:T(8,128)(2,1)} %bitcast.222), kind=kOutput, calls=%fused_computation.37 | convolution fusion | flops 4854906880 | bytes 22544384 | tf_op jit(solution)/shard_map/ecd,ecf->edf/dot_general | solution.py:263
  205.4 12.8 %convolution_convert_fusion.1 = bf16[8,1024,512]{2,1,0:T(8,128)(2,1)} fusion(bf16[8,576,512]{2,1,0:T(8,128)(2,1)} %get-tuple-element.77, bf16[8,288,1024]{2,1,0:T(8,128)(2,1)} %bitcast.227, bf16[8,288,1024]{2,1,0:T(8,128)(2,1)} %bitcast.223), kind=kOutput, calls=%fused_computation.36 | convolution fusion | flops 4854906880 | bytes 22544384 | tf_op jit(solution)/shard_map/ecd,ecf->edf/dot_general | solution.py:263
  218.3 18.4 %bitcast_convert_fusion = bf16[8,576,1024]{2,1,0:T(8,128)(2,1)} fusion(bf16[1,8,576,512]{3,2,1,0:T(8,128)(2,1)} %bitcast.183, bf16[1,8,576,512]{3,2,1,0:T(8,128)(2,1)} %bitcast.182, bf16[8,2,1024,512]{3,2,1,0:T(8,128)(2,1)} %param.22), kind=kOutput, calls=%fused_computation | convolution fusion | flops 9673113600 | bytes 35651584 | tf_op jit(solution)/shard_map/tecf,etdf->ecd/dot_general | solution.py:228
  236.7 6.0 bitcast_convert_fusion.1
  244.5 11.5 %convolution_convert_fusion = bf16[8,1024,512]{2,1,0:T(8,128)(2,1)} fusion(bf16[8,576,512]{2,1,0:T(8,128)(2,1)S(1)} %bitcast.181, bf16[8,288,1024]{2,1,0:T(8,128)(2,1)} %bitcast.219, bf16[8,288,1024]{2,1,0:T(8,128)(2,1)} %bitcast.217), kind=kOutput, calls=%fused_computation.35 | convolution fusion | flops 4854906880 | bytes 22544384 | tf_op jit(solution)/shard_map/ecd,ecf->edf/dot_general | solution.py:216
  256.1 6.5 fusion.24
  263.4 3.3 collective-permute-done.8
  266.7 3.8 multiply_reduce_fusion.1
  278.4 16.5 %fusion = (f32[8,2,512]{2,1,0:T(2,128)S(1)}, f32[8,512,512,2]{2,1,3,0:T(8,128)}) fusion(f32[1,8,2,512,512]{3,4,2,1,0:T(8,128)} %get-tuple-element.105, f32[8,2,512]{2,1,0:T(2,128)S(1)} %bitcast.202, bf16[512,8,64,1]{0,2,3,1:T(8,128)(2,1)} %bitcast.197, bf16[512,8,2,64]{0,3,2,1:T(8,128)(2,1)} %bitcast.175), kind=kOutput, calls=%fused_computation.5 | convolution fusion | flops 549445632 | bytes 35192832 | tf_op jit(solution)/shard_map/sqgjd,skgd->sgjqk/dot_general | solution.py:301
  295.0 11.1 %fusion.13 = bf16[8,2,512,512]{2,3,1,0:T(8,128)(2,1)} fusion(f32[8,512,512,2]{2,1,3,0:T(8,128)} %get-tuple-element.116, f32[1,8,2,512,512]{3,4,2,1,0:T(8,128)S(1)} %bitcast.174, f32[8,2,512]{2,1,0:T(2,128)S(1)} %get-tuple-element.115, f32[8,2,512]{2,1,0:T(2,128)S(1)} %bitcast.203), kind=kLoop, calls=%fused_computation.27 | loop fusion | flops 16777216 | bytes 42008576 | tf_op jit(solution)/shard_map/reshape.44
  306.1 7.2 fusion.64
  313.3 113.0 %all-reduce.5.cloned.1.call-done = bf16[8,1024,512]{2,1,0:T(8,128)(2,1)} async-done(((bf16[8,1024,512]{2,1,0:T(8,128)(2,1)}), bf16[8,1024,512]{2,1,0:T(8,128)(2,1)}) %all-reduce.5.cloned.1.call-update) | async-done | bytes 8388624 | tf_op jit(solution)/shard_map/psum | solution.py:219
  428.3 4.9 convolution_multiply_fusion
  434.4 9.8 %fusion.65 = bf16[8,64,512]{2,1,0:T(8,128)(2,1)S(1)} fusion(bf16[512,8,2,64]{0,3,2,1:T(8,128)(2,1)S(1)} %bitcast.176, f32[1,8,2,512,512]{3,4,2,1,0:T(8,128)} %get-tuple-element.105, f32[8,2,512]{2,1,0:T(2,128)S(1)} %bitcast.204), kind=kOutput, calls=%fused_computation.108 | convolution fusion | flops 545521664 | bytes 18382848 | tf_op jit(solution)/shard_map/sgjqk,sqgjd->skgd/dot_general | solution.py:298
  444.3 3.9 fusion.45
  448.7 2.6 convolution_convert_fusion.9
  451.3 4.6 convolution_convert_fusion.8
  455.9 10.9 %concatenate.68 = bf16[1024,3200]{1,0:T(8,128)(2,1)} concatenate(bf16[1024,2048]{1,0:T(8,128)(2,1)} %convolution_convert_fusion.8, bf16[1024,1024]{1,0:T(8,128)(2,1)} %convolution_convert_fusion.9, bf16[1024,16]{1,0:T(8,128)(2,1)S(1)} %copy.107, bf16[1024,1]{1,0:T(8,128)(2,1)S(1)} %convert_element_type.276, bf16[1024,1]{1,0:T(8,128)(2,1)S(1)} %convert_element_type.277, ...), dimensions={1} | concatenate | bytes 13107200 | tf_op jit(solution)/shard_map/concatenate | solution.py:334
  466.8 3.9 constant_dynamic-slice_fusion
  472.2 128.1 %all-reduce.7.cloned.1.call-done = bf16[8,1024,512]{2,1,0:T(8,128)(2,1)} async-done(((bf16[8,1024,512]{2,1,0:T(8,128)(2,1)}), bf16[8,1024,512]{2,1,0:T(8,128)(2,1)}) %all-reduce.7.cloned.1.call-update) | async-done | bytes 8388624 | tf_op jit(solution)/shard_map/psum | solution.py:266
  600.6 11.1 %convolution_convert_fusion.3 = bf16[8,576,1024]{2,1,0:T(8,128)(2,1)} fusion(bf16[8,576,512]{2,1,0:T(8,128)(2,1)} %get-tuple-element.79, bf16[8,1024,512]{2,1,0:T(8,128)(2,1)} %param.23), kind=kOutput, calls=%fused_computation.38 | convolution fusion | flops 4836556800 | bytes 22544384 | tf_op jit(solution)/shard_map/ecf,edf->ecd/dot_general | solution.py:231
  611.7 6.0 bitcast_convert_fusion.2
  619.1 4.5 fusion.42
  623.6 19.4 %collective-permute-done.6 = bf16[512,1024]{1,0:T(8,128)(2,1)} collective-permute-done((bf16[512,1024]{1,0:T(8,128)(2,1)}, bf16[512,1024]{1,0:T(8,128)(2,1)}, u32[]{:S(2)}, u32[]{:S(2)}) %collective-permute-start.6) | collective-permute-done | bytes 1048608 | tf_op jit(solution)/shard_map/ppermute | solution.py:66
  643.0 6.3 fusion.50
  649.3 12.0 %convert_element_type.273 = f32[8,1024,512]{2,1,0:T(8,128)} convert(bf16[8,1024,512]{2,1,0:T(8,128)(2,1)} %all-reduce.5.cloned.1.call-done) | non-fusion elementwise | flops 4194304 | bytes 25165824 | tf_op jit(solution)/shard_map/convert_element_type | solution.py:368
  661.3 5.4 add_convert_fusion
  666.7 107.2 %all-reduce.9.cloned.1.call-done = bf16[8,1024,512]{2,1,0:T(8,128)(2,1)} async-done(((bf16[8,1024,512]{2,1,0:T(8,128)(2,1)}), bf16[8,1024,512]{2,1,0:T(8,128)(2,1)}) %all-reduce.9.cloned.1.call-update) | async-done | bytes 8388624 | tf_op jit(solution)/shard_map/psum | solution.py:267
  773.9 8.4 maximum_convert_fusion
  782.3 11.5 %copy.111 = f32[8,2,1024,512]{3,2,1,0:T(8,128)} copy(f32[8,2,1024,512]{3,2,0,1:T(8,128)S(1)} %maximum_convert_fusion) | data formatting | bytes 67108864
  793.8 88.6 %all-reduce.11.cloned.1.call-done = bf16[512,3200]{1,0:T(8,128)(2,1)} async-done(((bf16[512,3200]{1,0:T(8,128)(2,1)}), bf16[512,3200]{1,0:T(8,128)(2,1)}) %all-reduce.11.cloned.1.call-update) | async-done | bytes 3276816 | tf_op jit(solution)/shard_map/psum | solution.py:354
  886.6 2.6 fusion.109
  (228 shorter events, 67.8 us)
Async XLA Ops:
  7.2 11.8 %copy-start.49 = (s32[512,8]{0,1:T(8,128)S(1)}, s32[512,8]{0,1:T(8,128)}, u32[]{:S(2)}) copy-start(s32[512,8]{0,1:T(8,128)} %param.13) | copy-start | bytes 49156
  7.2 12.6 %copy-start.4 = (bf16[512,1024]{1,0:T(8,128)(2,1)S(1)}, bf16[512,1024]{1,0:T(8,128)(2,1)}, u32[]{:S(2)}) copy-start(bf16[512,1024]{1,0:T(8,128)(2,1)} %param.12) | copy-start | bytes 3145732
  7.2 419.1 %all-reduce.5.cloned.1.call-start = ((), (), s32[]{:S(2)}) async-start(), calls=%async_computation | async-start | bytes 16777216 | tf_op jit(solution)/shard_map/psum | solution.py:219
  16.0 28.1 %collective-permute-start = (bf16[256,2176]{1,0:T(8,128)(2,1)}, bf16[256,2176]{1,0:T(8,128)(2,1)}, u32[]{:S(2)}, u32[]{:S(2)}) collective-permute-start(bf16[256,2176]{1,0:T(8,128)(2,1)} %constant_dynamic-slice_fusion.2), channel_id=1, source_target_pairs={{0,16},{16,0},{1,17},{17,1},{2,18},{18,2},{3,19},{19,3},{4,20},{20... | collective-permute-start | bytes 3342344 | tf_op jit(solution)/shard_map/ppermute | solution.py:66
  18.9 25.1 %collective-permute-start.4 = (s32[512,8]{0,1:T(8,128)S(1)}, s32[512,8]{0,1:T(8,128)S(1)}, u32[]{:S(2)}, u32[]{:S(2)}) collective-permute-start(s32[512,8]{0,1:T(8,128)S(1)} %copy-done.49), channel_id=1, source_target_pairs={{0,16},{16,0},{1,17},{17,1},{2,18},{18,2},{3,19},{19,3},{4,20},{20... | collective-permute-start | bytes 49160 | tf_op jit(solution)/shard_map/ppermute | solution.py:66
  20.7 62.0 %copy-start.51 = (f32[512]{0:T(512)}, f32[512]{0:T(512)S(1)}, u32[]{:S(2)}) copy-start(f32[512]{0:T(512)S(1)} %get-tuple-element.99) | copy-start | bytes 6148
  23.7 40.6 %copy-start.20 = (f32[512,32]{0,1:T(8,128)}, f32[512,32]{0,1:T(8,128)S(1)}, u32[]{:S(2)}) copy-start(f32[512,32]{0,1:T(8,128)S(1)} %get-tuple-element.102) | copy-start | bytes 196612
  23.7 40.6 %copy-start.22 = (f32[512,32]{0,1:T(8,128)}, f32[512,32]{0,1:T(8,128)S(1)}, u32[]{:S(2)}) copy-start(f32[512,32]{0,1:T(8,128)S(1)} %get-tuple-element.103) | copy-start | bytes 196612
  44.1 12.0 %collective-permute-start.1 = (bf16[256,2176]{1,0:T(8,128)(2,1)}, bf16[256,2176]{1,0:T(8,128)(2,1)S(1)}, u32[]{:S(2)}, u32[]{:S(2)}) collective-permute-start(bf16[256,2176]{1,0:T(8,128)(2,1)} %collective-permute-done), channel_id=1, source_target_pairs={{0,1},{1,0},{2,3},{3,2},{4,5},{5,4},{6,7},{7,6},{8,9},{9,8},{10,11... | collective-permute-start | bytes 3342344 | tf_op jit(solution)/shard_map/ppermute | solution.py:85
  58.8 23.9 %copy-start.47 = (f32[1024,1]{0,1:T(1,128)}, f32[1024,1]{0,1:T(1,128)S(1)}, u32[]{:S(2)}) copy-start(f32[1024,1]{0,1:T(1,128)S(1)} %get-tuple-element.81) | copy-start | bytes 12292
  58.8 37.0 %copy-start.39 = (f32[1024,1]{0,1:T(1,128)}, f32[1024,1]{0,1:T(1,128)S(1)}, u32[]{:S(2)}) copy-start(f32[1024,1]{0,1:T(1,128)S(1)} %get-tuple-element.80) | copy-start | bytes 12292
  64.3 10.2 %copy-start.16 = (bf16[1,512,16,32]{1,3,2,0:T(8,128)(2,1)}, bf16[1,512,16,32]{1,3,2,0:T(8,128)(2,1)S(1)}, u32[]{:S(2)}) copy-start(bf16[1,512,16,32]{1,3,2,0:T(8,128)(2,1)S(1)} %get-tuple-element.88) | copy-start | bytes 1572868
  64.3 10.2 %copy-start.18 = (bf16[1,512,16,32]{1,3,2,0:T(8,128)(2,1)}, bf16[1,512,16,32]{1,3,2,0:T(8,128)(2,1)S(1)}, u32[]{:S(2)}) copy-start(bf16[1,512,16,32]{1,3,2,0:T(8,128)(2,1)S(1)} %get-tuple-element.89) | copy-start | bytes 1572868
  64.5 10.0 %copy-start.28 = (bf16[512,8,32]{0,2,1:T(8,128)(2,1)}, bf16[512,8,32]{0,2,1:T(8,128)(2,1)S(1)}, u32[]{:S(2)}) copy-start(bf16[512,8,32]{0,2,1:T(8,128)(2,1)S(1)} %get-tuple-element.92) | copy-start | bytes 786436
  64.5 10.0 %copy-start.30 = (bf16[512,8,32]{0,2,1:T(8,128)(2,1)}, bf16[512,8,32]{0,2,1:T(8,128)(2,1)S(1)}, u32[]{:S(2)}) copy-start(bf16[512,8,32]{0,2,1:T(8,128)(2,1)S(1)} %get-tuple-element.93) | copy-start | bytes 786436
  64.6 20.2 %collective-permute-start.2 = (bf16[256,1024]{1,0:T(8,128)(2,1)S(1)}, bf16[256,1024]{1,0:T(8,128)(2,1)S(1)}, u32[]{:S(2)}, u32[]{:S(2)}) collective-permute-start(bf16[256,1024]{1,0:T(8,128)(2,1)S(1)} %constant_dynamic-slice_fusion.1), channel_id=1, source_target_pairs={{0,16},{16,0},{1,17},{17,1},{2,18},{18,2},{3,19},{19,3},{4,20},{20... | collective-permute-start | bytes 1572872 | tf_op jit(solution)/shard_map/ppermute | solution.py:66
  84.8 8.9 collective-permute-start.3
  96.8 26.1 %collective-permute-start.5 = (bf16[512,1024]{1,0:T(8,128)(2,1)S(1)}, bf16[512,1024]{1,0:T(8,128)(2,1)S(1)}, u32[]{:S(2)}, u32[]{:S(2)}) collective-permute-start(bf16[512,1024]{1,0:T(8,128)(2,1)S(1)} %multiply_convert_fusion.4), channel_id=1, source_target_pairs={{0,16},{16,0},{1,17},{17,1},{2,18},{18,2},{3,19},{19,3},{4,20},{20... | collective-permute-start | bytes 3145736 | tf_op jit(solution)/shard_map/ppermute | solution.py:66
  97.2 50.8 %collective-permute-start.7 = (bf16[512,1024]{1,0:T(8,128)(2,1)S(1)}, bf16[512,1024]{1,0:T(8,128)(2,1)S(1)}, u32[]{:S(2)}, u32[]{:S(2)}) collective-permute-start(bf16[512,1024]{1,0:T(8,128)(2,1)S(1)} %copy-done.27), channel_id=1, source_target_pairs={{0,16},{16,0},{1,17},{17,1},{2,18},{18,2},{3,19},{19,3},{4,20},{20... | collective-permute-start | bytes 3145736 | tf_op jit(solution)/shard_map/ppermute | solution.py:66
  100.2 22.7 %copy-start.24 = (pred[2304,512]{1,0:T(32,128)(4,1)S(1)}, pred[2304,512]{1,0:T(32,128)(4,1)}, u32[]{:S(2)}) copy-start(pred[2304,512]{1,0:T(32,128)(4,1)} %get-tuple-element.97) | copy-start | bytes 3538948
  103.1 34.4 %copy-start.54 = (bf16[2304,1024]{1,0:T(8,128)(2,1)}, bf16[2304,1024]{1,0:T(8,128)(2,1)S(1)}, u32[]{:S(2)}) copy-start(bf16[2304,1024]{1,0:T(8,128)(2,1)S(1)} %convolution_convert_fusion.7) | copy-start | bytes 14155780
  173.9 88.6 %collective-permute-start.9 = (f32[8,512]{1,0:T(8,128)S(1)}, f32[8,512]{1,0:T(8,128)S(1)}, u32[]{:S(2)}, u32[]{:S(2)}) collective-permute-start(f32[8,512]{1,0:T(8,128)S(1)} %get-tuple-element.71), channel_id=1, source_target_pairs={{0,16},{16,0},{1,17},{17,1},{2,18},{18,2},{3,19},{19,3},{4,20},{20... | collective-permute-start | bytes 49160 | tf_op jit(solution)/shard_map/ppermute | solution.py:66
  205.4 39.0 %slice-start.4 = ((s8[4718592]{0:T(1024)(128)(4,1)}), s8[524288]{0:T(1024)(128)(4,1)S(1)}, s32[]{:S(2)}) async-start(s8[4718592]{0:T(1024)(128)(4,1)} %bitcast.180), calls=%async_computation.8 | async-start | bytes 1048576
  218.3 26.2 %slice-start.5 = ((s8[4718592]{0:T(1024)(128)(4,1)}), s8[4194304]{0:T(1024)(128)(4,1)S(1)}, s32[]{:S(2)}) async-start(s8[4718592]{0:T(1024)(128)(4,1)} %bitcast.180), calls=%async_computation.9 | async-start | bytes 8388608
  242.7 24.0 %collective-permute-start.8 = (bf16[512,1024]{1,0:T(8,128)(2,1)}, bf16[512,1024]{1,0:T(8,128)(2,1)}, u32[]{:S(2)}, u32[]{:S(2)}) collective-permute-start(bf16[512,1024]{1,0:T(8,128)(2,1)} %bitcast_convert_fusion.1), channel_id=1, source_target_pairs={{0,16},{16,0},{1,17},{17,1},{2,18},{18,2},{3,19},{19,3},{4,20},{20... | collective-permute-start | bytes 3145736 | tf_op jit(solution)/shard_map/ppermute | solution.py:66
  256.0 10.7 %copy-start.1 = (f32[512,1024]{1,0:T(8,128)S(1)}, f32[512,1024]{1,0:T(8,128)}, u32[]{:S(2)}) copy-start(f32[512,1024]{1,0:T(8,128)} %copy-done) | copy-start | bytes 6291460
  256.0 10.7 %copy-start.40 = (f32[1024,1]{0,1:T(1,128)S(1)}, f32[1024,1]{0,1:T(1,128)}, u32[]{:S(2)}) copy-start(f32[1024,1]{0,1:T(1,128)} %copy-done.39) | copy-start | bytes 12292
  256.0 10.7 %copy-start.44 = (f32[512]{0:T(512)S(1)}, f32[512]{0:T(512)}, u32[]{:S(2)}) copy-start(f32[512]{0:T(512)} %copy-done.43) | copy-start | bytes 6148
  256.0 344.3 %all-reduce.7.cloned.1.call-start = ((), (), s32[]{:S(2)}) async-start(), calls=%async_computation.1 | async-start | bytes 16777216 | tf_op jit(solution)/shard_map/psum | solution.py:266
  278.4 16.5 %slice-start = ((s8[16777216]{0:T(1024)(128)(4,1)}), s8[4194304]{0:T(1024)(128)(4,1)S(1)}, s32[]{:S(2)}) async-start(s8[16777216]{0:T(1024)(128)(4,1)} %bitcast.173), calls=%async_computation.4 | async-start | bytes 8388608
  278.4 16.5 %slice-start.1 = ((s8[16777216]{0:T(1024)(128)(4,1)}), s8[4194304]{0:T(1024)(128)(4,1)S(1)}, s32[]{:S(2)}) async-start(s8[16777216]{0:T(1024)(128)(4,1)} %bitcast.173), calls=%async_computation.5 | async-start | bytes 8388608
  278.4 16.5 %slice-start.2 = ((s8[16777216]{0:T(1024)(128)(4,1)}), s8[4194304]{0:T(1024)(128)(4,1)S(1)}, s32[]{:S(2)}) async-start(s8[16777216]{0:T(1024)(128)(4,1)} %bitcast.173), calls=%async_computation.6 | async-start | bytes 8388608
  278.4 16.5 %slice-start.3 = ((s8[16777216]{0:T(1024)(128)(4,1)}), s8[4194304]{0:T(1024)(128)(4,1)S(1)}, s32[]{:S(2)}) async-start(s8[16777216]{0:T(1024)(128)(4,1)} %bitcast.173), calls=%async_computation.7 | async-start | bytes 8388608
  295.0 11.1 %copy-start.17 = (bf16[1,512,16,32]{1,3,2,0:T(8,128)(2,1)S(1)}, bf16[1,512,16,32]{1,3,2,0:T(8,128)(2,1)}, u32[]{:S(2)}) copy-start(bf16[1,512,16,32]{1,3,2,0:T(8,128)(2,1)} %copy-done.16) | copy-start | bytes 1572868
  295.0 11.1 %copy-start.19 = (bf16[1,512,16,32]{1,3,2,0:T(8,128)(2,1)S(1)}, bf16[1,512,16,32]{1,3,2,0:T(8,128)(2,1)}, u32[]{:S(2)}) copy-start(bf16[1,512,16,32]{1,3,2,0:T(8,128)(2,1)} %copy-done.18) | copy-start | bytes 1572868
  313.3 113.5 %copy-start.21 = (f32[512,32]{0,1:T(8,128)S(1)}, f32[512,32]{0,1:T(8,128)}, u32[]{:S(2)}) copy-start(f32[512,32]{0,1:T(8,128)} %copy-done.20) | copy-start | bytes 196612
  313.3 113.5 %copy-start.23 = (f32[512,32]{0,1:T(8,128)S(1)}, f32[512,32]{0,1:T(8,128)}, u32[]{:S(2)}) copy-start(f32[512,32]{0,1:T(8,128)} %copy-done.22) | copy-start | bytes 196612
  313.3 115.0 %copy-start.29 = (bf16[512,8,32]{0,2,1:T(8,128)(2,1)S(1)}, bf16[512,8,32]{0,2,1:T(8,128)(2,1)}, u32[]{:S(2)}) copy-start(bf16[512,8,32]{0,2,1:T(8,128)(2,1)} %copy-done.28) | copy-start | bytes 786436
  313.3 115.0 %copy-start.31 = (bf16[512,8,32]{0,2,1:T(8,128)(2,1)S(1)}, bf16[512,8,32]{0,2,1:T(8,128)(2,1)}, u32[]{:S(2)}) copy-start(bf16[512,8,32]{0,2,1:T(8,128)(2,1)} %copy-done.30) | copy-start | bytes 786436
  426.4 347.5 %all-reduce.9.cloned.1.call-start = ((), (), s32[]{:S(2)}) async-start(), calls=%async_computation.2 | async-start | bytes 16777216 | tf_op jit(solution)/shard_map/psum | solution.py:267
  433.2 11.1 %slice-start.6 = ((s8[4456448]{0:T(1024)(128)(4,1)}), s8[4194304]{0:T(1024)(128)(4,1)S(1)}, s32[]{:S(2)}) async-start(s8[4456448]{0:T(1024)(128)(4,1)} %bitcast.184), calls=%async_computation.10 | async-start | bytes 8388608
  434.4 9.9 %copy-start.5 = (bf16[512,1024]{1,0:T(8,128)(2,1)S(1)}, bf16[512,1024]{1,0:T(8,128)(2,1)}, u32[]{:S(2)}) copy-start(bf16[512,1024]{1,0:T(8,128)(2,1)} %param.12) | copy-start | bytes 3145732
  434.4 9.9 %slice-start.7 = ((s8[4456448]{0:T(1024)(128)(4,1)}), s8[262144]{0:T(1024)(128)(4,1)S(1)}, s32[]{:S(2)}) async-start(s8[4456448]{0:T(1024)(128)(4,1)} %bitcast.184), calls=%async_computation.11 | async-start | bytes 524288
  434.4 9.9 %copy-start.48 = (f32[1024,1]{0,1:T(1,128)S(1)}, f32[1024,1]{0,1:T(1,128)}, u32[]{:S(2)}) copy-start(f32[1024,1]{0,1:T(1,128)} %copy-done.47) | copy-start | bytes 12292
  434.4 9.9 %copy-start.52 = (f32[512]{0:T(512)S(1)}, f32[512]{0:T(512)}, u32[]{:S(2)}) copy-start(f32[512]{0:T(512)} %copy-done.51) | copy-start | bytes 6148
  470.7 190.5 %collective-permute-start.10 = (bf16[512,3200]{1,0:T(8,128)(2,1)}, bf16[512,3200]{1,0:T(8,128)(2,1)}, u32[]{:S(2)}, u32[]{:S(2)}) collective-permute-start(bf16[512,3200]{1,0:T(8,128)(2,1)} %constant_dynamic-slice_fusion), channel_id=1, source_target_pairs={{0,16},{16,0},{1,17},{17,1},{2,18},{18,2},{3,19},{19,3},{4,20},{20... | collective-permute-start | bytes 9830408 | tf_op jit(solution)/shard_map/ppermute | solution.py:66
  600.3 282.1 %all-reduce.11.cloned.1.call-start = ((), (), s32[]{:S(2)}) async-start(), calls=%async_computation.3 | async-start | bytes 6553600 | tf_op jit(solution)/shard_map/psum | solution.py:354
  617.7 25.3 %collective-permute-start.6 = (bf16[512,1024]{1,0:T(8,128)(2,1)}, bf16[512,1024]{1,0:T(8,128)(2,1)}, u32[]{:S(2)}, u32[]{:S(2)}) collective-permute-start(bf16[512,1024]{1,0:T(8,128)(2,1)} %bitcast_convert_fusion.2), channel_id=1, source_target_pairs={{0,16},{16,0},{1,17},{17,1},{2,18},{18,2},{3,19},{19,3},{4,20},{20... | collective-permute-start | bytes 3145736 | tf_op jit(solution)/shard_map/ppermute | solution.py:66
  (30 other events, 125.7 us)
Sparse Core Ops, SparseCore 0:
  256.1 170.2 all-reduce.4
  430.5 169.7 all-reduce.6
  604.1 169.7 all-reduce.8
  777.8 104.5 all-reduce.10

commit v2 on v1

--- a/solution.py
+++ b/solution.py
@@ -86,6 +86,31 @@
         whole = lax.dynamic_update_slice_in_dim(whole, first, owner * rows + odd * half, 0)
         whole = lax.dynamic_update_slice_in_dim(whole, second, owner * rows + (1 - odd) * half, 0)
     return whole
+
+
+def flip(value, size, bit):
+    return lax.ppermute(value, "rep", [(i, i ^ (1 << bit)) for i in range(size)])
+
+
+def halve(block, reps, bit):
+    half = block.shape[0] // 2
+    odd = (lax.axis_index("rep") >> bit) & 1
+    given = lax.dynamic_slice_in_dim(block, (1 - odd) * half, half, 0)
+    kept = lax.dynamic_slice_in_dim(block, odd * half, half, 0)
+    taken = flip(given, reps, bit)
+    return (kept.astype(jnp.float32) + taken.astype(jnp.float32)).astype(block.dtype)
+
+
+def ordered(block, taken, bit, kind):
+    odd = (lax.axis_index("rep") >> bit) & 1
+    half = block.shape[0]
+    whole = jnp.zeros((2 * half,) + block.shape[1:], kind)
+    whole = lax.dynamic_update_slice_in_dim(whole, block.astype(kind), odd * half, 0)
+    return lax.dynamic_update_slice_in_dim(whole, taken.astype(kind), (1 - odd) * half, 0)
+
+
+def double(block, reps, bit):
+    return ordered(block, flip(block, reps, bit), bit, block.dtype)
 
 
 def per_device(
@@ -204,6 +229,14 @@
     grads_in = jnp.concatenate(grad_slots, 1)
     slot_gate = jnp.concatenate(gate_slots, 1)[:, :, None] * RESIDUAL_SCALE
 
+    bits = reps.bit_length() - 1
+
+    def step_down(block, bit):
+        return halve(block, reps, bit) if bit < bits else block
+
+    def step_up(block, bit):
+        return double(block, reps, bit) if bit < bits else block
+
     def up(part):
         return jnp.einsum(
             "ecd,edf->ecf", rows_in, expert_in[:, part], preferred_element_type=jnp.float32
@@ -216,18 +249,37 @@
     out_term = jnp.einsum(
         "ecd,ecf->edf", grads_in, scaled_hidden, preferred_element_type=jnp.float32
     ).astype(low)
-    out_total = lax.psum(out_term, "rep")
+    out_sum = halve(out_term.reshape(-1, out_term.shape[-1]), reps, 0)
     hidden_grad = jnp.einsum(
-        "ecd,edf->ecf", grads_in, expert_out, preferred_element_type=jnp.float32
+        "ecd,edf->ecf", after(grads_in, out_term), expert_out, preferred_element_type=jnp.float32
     )
     gate_grad_slots = RESIDUAL_SCALE * jnp.sum(hidden * hidden_grad, -1)
     hidden_grad = slot_gate * hidden_grad
     gate_side = (hidden_grad * up_act * sigmoid * (1.0 + gate_act * (1.0 - sigmoid))).astype(low)
     up_side = (hidden_grad * (gate_act * sigmoid)).astype(low)
-    pair_side = jnp.stack([gate_side, up_side])
+    gate_side, up_side, out_sum = lax.optimization_barrier((gate_side, up_side, out_sum))
+    out_sum = step_down(out_sum, 1)
+    in_terms = [
+        jnp.einsum("ecd,ecf->edf", rows_in, part, preferred_element_type=jnp.float32).astype(low)
+        for part in (gate_side, up_side)
+    ]
+    gate_later, up_later, out_sum, gate_term, up_term = lax.optimization_barrier(
+        (gate_side, up_side, out_sum, in_terms[0], in_terms[1])
+    )
+    gate_sum = halve(gate_term.reshape(-1, gate_term.shape[-1]), reps, 0)
+    up_sum = halve(up_term.reshape(-1, up_term.shape[-1]), reps, 0)
+    out_sum = step_down(out_sum, 2)
+    pair_side = jnp.stack([gate_later, up_later])
     rows_grad = jnp.einsum(
         "tecf,etdf->ecd", pair_side, expert_in, preferred_element_type=jnp.float32
     ).astype(low)
+    rows_grad, gate_sum, up_sum, out_sum = lax.optimization_barrier(
+        (rows_grad, gate_sum, up_sum, out_sum)
+    )
+    gate_sum, out_sum = step_down(gate_sum, 1), step_down(out_sum, 3)
+    for bit in range(4, bits):
+        out_sum = halve(out_sum, reps, bit)
+    up_sum = step_down(up_sum, 1)
     mixed = jnp.einsum(
         "ecf,edf->ecd", scaled_hidden, expert_out, preferred_element_type=jnp.float32
     ).astype(low)
@@ -259,13 +311,6 @@
         gate_grad_parts.append(gate_part)
     layer_out = (residual + mix).astype(low)
 
-    in_terms = [
-        jnp.einsum("ecd,ecf->edf", rows_in, part, preferred_element_type=jnp.float32).astype(low)
-        for part in (gate_side, up_side)
-    ]
-    gate_total = lax.psum(after(in_terms[0], out_total), "rep")
-    up_total = lax.psum(after(in_terms[1], gate_total), "rep")
-
     gate_grad = jnp.zeros((EXPERTS, row_count), jnp.float32)
     for k in range(shards):
         start = lax.rem(me + k, shards) * local
@@ -279,6 +324,10 @@
         logit_grad, router_full.astype(jnp.float32).T, precision=exact
     )
     router_term = jnp.dot(normed_two.astype(jnp.float32).T, logit_grad, precision=exact)
+    norm_grad_two, gate_sum, out_sum = lax.optimization_barrier((norm_grad_two, gate_sum, out_sum))
+    for bit in reversed(range(3, bits)):
+        out_sum = double(out_sum, reps, bit)
+    gate_sum = step_down(gate_sum, 2)
     weighted_two = gain_two * norm_grad_two
     gain_two_term = jnp.sum(norm_grad_two * residual * scale_two, 0)
     residual_grad = (
@@ -304,6 +353,12 @@
     score_grad = (
         probs_f * (prob_grad - jnp.sum(probs_f * prob_grad, -1, keepdims=True))
     ).astype(low)
+    score_grad, up_sum, gate_sum, out_sum = lax.optimization_barrier(
+        (score_grad, up_sum, gate_sum, out_sum)
+    )
+    out_sum, up_sum = step_up(out_sum, 2), step_down(up_sum, 2)
+    for bit in range(3, bits):
+        gate_sum = halve(gate_sum, reps, bit)
     query_grad = ATTN_SCALE * jnp.einsum(
         "sgjqk,skgd->sqgjd", score_grad, keys_low, preferred_element_type=jnp.float32
     )
@@ -320,6 +375,14 @@
         ],
         1,
     )
+    qkv_low, gate_sum, up_sum, out_sum = lax.optimization_barrier(
+        (qkv_low, gate_sum, up_sum, out_sum)
+    )
+    out_sum = step_up(out_sum, 1)
+    for bit in range(3, bits):
+        up_sum = halve(up_sum, reps, bit)
+    for bit in reversed(range(2, bits)):
+        gate_sum = double(gate_sum, reps, bit)
     qkv_term = jnp.einsum("td,tq->dq", normed_one, qkv_low, preferred_element_type=jnp.float32)
     norm_grad_one = jnp.einsum(
         "tq,dq->td", qkv_low, qkv_full, preferred_element_type=jnp.float32
@@ -350,8 +413,29 @@
     share = rows_for(0).astype(jnp.float32)
     for k in range(1, shards):
         share = share + shift(rows_for(k), "shard", shards, k)
-    share = after(share.astype(low), up_total)
-    total = lax.psum(share, "rep").astype(jnp.float32)
+    share = share.astype(low)
+    for bit in range(bits):
+        share = halve(share, reps, bit)
+    for bit in reversed(range(bits)):
+        share = double(share, reps, bit)
+    total = share.astype(jnp.float32)
+    for bit in reversed(range(2, bits)):
+        up_sum = double(up_sum, reps, bit)
+    gate_sum, up_sum = step_up(gate_sum, 1), step_up(up_sum, 1)
+
+    def blocks(value):
+        return value.reshape(-1, D, value.shape[-1])
+
+    odd = lax.rem(lax.axis_index("rep"), 2)
+    in_total = jnp.zeros((local, 2, D, gate_sum.shape[-1]), jnp.float32)
+    for part, value in enumerate((gate_sum, up_sum)):
+        for place, piece in ((odd, value), (1 - odd, flip(value, reps, 0))):
+            in_total = lax.dynamic_update_slice(
+                in_total,
+                blocks(piece)[:, None].astype(jnp.float32),
+                (place * (local // 2), part, 0, 0),
+            )
+    out_total = blocks(ordered(out_sum, flip(out_sum, reps, 0), 0, jnp.float32))
     base = query_width + 2 * kv_width
     side = total[:, base + D :]
     return (
@@ -364,8 +448,8 @@
         side[:, EXPERTS],
         side[:, EXPERTS + 1],
         side[:, :EXPERTS],
-        jnp.stack([gate_total, up_total], 1).astype(jnp.float32),
-        out_total.astype(jnp.float32),
+        in_total,
+        out_total,
     )
 
 

time: 906 us -> 901 us (level)
  waiting for transfers between devices: 496 us -> 396 us
  local copies, waits for them, and re-layouts: 61.1 us -> 126 us
  starting transfers between devices: 13 us -> 42.6 us
  other arithmetic: 82.8 us -> 103 us
  between operations: 15 us -> 2.95 us
    psum x4 -> x0, waiting for transfers between devices: 437 us -> none  [the longest x1 128 us: per_device(): gate_total = lax.psum(after(in_terms[0], out_total), 'rep')]
    ppermute x0 -> x32, waiting for transfers between devices: none -> 275 us  [flip(): return lax.ppermute(value, 'rep', [(i, i ^ 1 << bit) for i in range(size)])]
    ppermute x9, waiting for transfers between devices: 59.2 us -> 121 us  [shift(): lax.ppermute(value, axis, [(i, (i + step) % size) for i in range(size)])]
    dynamic_update_slice x0 -> x8, other arithmetic: none -> 38.9 us  [the longest x4 27.1 us: per_device(): lax.dynamic_update_slice(in_total, blocks(piece)[:, None].astype(jnp.floa...]
    ppermute x0 -> x32, starting transfers between devices: none -> 31.3 us  [flip(): return lax.ppermute(value, 'rep', [(i, i ^ 1 << bit) for i in range(size)])]
    dynamic_update_slice x0 -> x25, local copies, waits for them, and re-layouts: none -> 27.6 us  [the longest x14 16.1 us: ordered(): lax.dynamic_update_slice_in_dim(whole, taken.astype(kind), (1 - odd) * ha...]
    dynamic_slice x0 -> x16, local copies, waits for them, and re-layouts: none -> 16 us  [halve(): given = lax.dynamic_slice_in_dim(block, (1 - odd) * half, half, 0)]
    broadcast_in_dim x0 -> x6, local copies, waits for them, and re-layouts: none -> 14.1 us  [the longest x1 11.5 us: per_device(): in_total = jnp.zeros((local, 2, D, gate_sum.shape[-1]), jnp.float32)]
  transfers between devices with their start and end apart: 15 -> 43, of which waited for: 8 -> 21; matrix products, arithmetic and copies ran while one was open for 35% -> 38% of each run, Pallas kernels for 0% -> 0%
where the time goes in v2:
time: 901 us; the launch traced here: 892 us
  waiting for transfers between devices  396 us (44%)
  matrix products  221 us (25%)
  local copies, waits for them, and re-layouts  126 us (14%)
  other arithmetic  103 us (11%)
  starting transfers between devices  42.6 us (5%)
    ppermute x32, waiting for transfers between devices, flip(): return lax.ppermute(value, 'rep', [(i, i ^ 1 << bit) for i in range(size)])  275 us
    ppermute x9, waiting for transfers between devices, shift(): lax.ppermute(value, axis, [(i, (i + step) % size) for i in range(size)])  121 us
    ppermute x32, starting transfers between devices, flip(): return lax.ppermute(value, 'rep', [(i, i ^ 1 << bit) for i in range(size)])  31.3 us
    dynamic_update_slice x4, other arithmetic, per_device(): lax.dynamic_update_slice(in_total, blocks(piece)[:, None].astype(jnp.floa...  27.1 us
    dot_general x2, matrix products, per_device(): jnp.einsum('ecd,ecf->edf', rows_in, part, preferred_element_type=jnp.floa...  25.7 us
    convert_element_type x14, other arithmetic, halve(): (kept.astype(jnp.float32) + taken.astype(jnp.float32)).astype(block.dtype)  22.8 us
    dot_general x2, matrix products, up(): jnp.einsum('ecd,edf->ecf', rows_in, expert_in[:, part], preferred_element...  20.8 us
    dot_general x4, matrix products, collect(): jnp.einsum('st,sd->td', spread, values[:, span].reshape(local * CAP, D),...  20.8 us
  transfers between devices with their start and end apart: 43, of which 21 were waited for; matrix products, arithmetic and copies ran while one was open for 38% of the time, Pallas kernels for 0%

profile of v2, /device:TPU:0, one launch (start us, length us, event | category | flops | bytes accessed | tf_op | source)
XLA Modules:
  0.0 892.3 jit_solution(17511252971351489825)
XLA Ops:
  20.7 16.8 %collective-permute-done.4 = s32[512,8]{0,1:T(8,128)S(1)} collective-permute-done((s32[512,8]{0,1:T(8,128)S(1)}, s32[512,8]{0,1:T(8,128)S(1)}, u32[]{:S(2)}, u32[]{:S(2)}) %collective-permute-start.4) | collective-permute-done | bytes 16416 | tf_op jit(solution)/shard_map/ppermute | solution.py:66
  41.3 5.4 convolution_convert_fusion.5
  59.7 7.8 fusion.128
  67.6 8.2 fusion.3
  78.1 7.5 fusion.63
  96.8 19.1 %collective-permute-done.5 = bf16[512,1024]{1,0:T(8,128)(2,1)S(1)} collective-permute-done((bf16[512,1024]{1,0:T(8,128)(2,1)S(1)}, bf16[512,1024]{1,0:T(8,128)(2,1)S(1)}, u32[]{:S(2)}, u32[]{:S(2)}) %collective-permute-start.5) | collective-permute-done | bytes 1048608 | tf_op jit(solution)/shard_map/ppermute | solution.py:66
  118.7 11.3 %fusion.13 = f32[8,576,512]{2,1,0:T(8,128)} fusion(bf16[8,288,1024]{2,1,0:T(8,128)(2,1)S(1)} %bitcast.252, bf16[8,288,1024]{2,1,0:T(8,128)(2,1)S(1)} %bitcast.248, bf16[8,2,1024,512]{3,2,1,0:T(8,128)(2,1)} %param.22), kind=kOutput, calls=%fused_computation.27 | convolution fusion | flops 4850712576 | bytes 27262976 | tf_op jit(solution)/shard_map/ecd,edf->ecf/dot_general | solution.py:241
  130.0 9.5 %fusion.14 = f32[8,576,512]{2,1,0:T(8,128)} fusion(bf16[8,288,1024]{2,1,0:T(8,128)(2,1)S(1)} %bitcast.253, bf16[8,288,1024]{2,1,0:T(8,128)(2,1)S(1)} %bitcast.249, bf16[8,2,1024,512]{3,2,1,0:T(8,128)(2,1)} %param.22), kind=kOutput, calls=%fused_computation.29 | convolution fusion | flops 4850712576 | bytes 27262976 | tf_op jit(solution)/shard_map/ecd,edf->ecf/dot_general | solution.py:241
  150.6 14.9 %convolution_convert_fusion.2 = bf16[8,1024,512]{2,1,0:T(8,128)(2,1)} fusion(f32[8,576]{1,0:T(8,128)S(1)} %maximum_multiply_fusion, bf16[8,288,1024]{2,1,0:T(8,128)(2,1)} %bitcast.214, bf16[8,288,1024]{2,1,0:T(8,128)(2,1)} %bitcast.209, f32[8,576,512]{2,1,0:T(8,128)} %fusion.13, f32[8,576,512]{2,1,0:T(8,128)} %fusion.14), kind=kOutput, calls=%fused_computation.48 | convolution fusion | flops 4871421952 | bytes 36718592 | tf_op jit(solution)/shard_map/ecd,ecf->edf/dot_general | solution.py:249
  169.9 18.7 %multiply_reduce_fusion = (f32[8,576]{1,0:T(8,128)S(1)}, bf16[8,576,512]{2,1,0:T(8,128)(2,1)}, bf16[8,576,512]{2,1,0:T(8,128)(2,1)}) fusion(f32[8,576,512]{2,1,0:T(8,128)} %fusion.13, f32[8,576,512]{2,1,0:T(8,128)} %fusion.14, f32[8,576]{1,0:T(8,128)S(1)} %maximum_multiply_fusion, bf16[8,576,1024]{2,1,0:T(8,128)(2,1)} %pad_maximum_fusion.1, ...), kind=kOutput, calls=%fused_computation.18 | convolution fusion | flops 4871941632 | bytes 46174208 | tf_op jit(solution)/shard_map/ecd,edf->ecf/dot_general | solution.py:253
  188.7 14.3 %convolution_convert_fusion.3 = bf16[8,576,1024]{2,1,0:T(8,128)(2,1)} fusion(bf16[8,1024,512]{2,1,0:T(8,128)(2,1)} %param.23, f32[8,576]{1,0:T(8,128)S(1)} %maximum_multiply_fusion, f32[8,576,512]{2,1,0:T(8,128)} %fusion.13, f32[8,576,512]{2,1,0:T(8,128)} %fusion.14), kind=kOutput, calls=%fused_computation.49 | convolution fusion | flops 4853071872 | bytes 36718592 | tf_op jit(solution)/shard_map/ecf,edf->ecd/dot_general | solution.py:283
  209.4 12.8 %convolution_convert_fusion.1 = bf16[8,1024,512]{2,1,0:T(8,128)(2,1)} fusion(bf16[8,576,512]{2,1,0:T(8,128)(2,1)} %get-tuple-element.43, bf16[8,288,1024]{2,1,0:T(8,128)(2,1)} %bitcast.254, bf16[8,288,1024]{2,1,0:T(8,128)(2,1)} %bitcast.250), kind=kOutput, calls=%fused_computation.47 | convolution fusion | flops 4854906880 | bytes 22544384 | tf_op jit(solution)/shard_map/ecd,ecf->edf/dot_general | solution.py:263
  222.2 12.9 %convolution_convert_fusion = bf16[8,1024,512]{2,1,0:T(8,128)(2,1)} fusion(bf16[8,576,512]{2,1,0:T(8,128)(2,1)} %get-tuple-element.44, bf16[8,288,1024]{2,1,0:T(8,128)(2,1)} %bitcast.255, bf16[8,288,1024]{2,1,0:T(8,128)(2,1)} %bitcast.251), kind=kOutput, calls=%fused_computation.46 | convolution fusion | flops 4854906880 | bytes 22544384 | tf_op jit(solution)/shard_map/ecd,ecf->edf/dot_general | solution.py:263
  235.1 20.8 %collective-permute-done.9 = bf16[2048,512]{1,0:T(8,128)(2,1)S(1)} collective-permute-done((bf16[2048,512]{1,0:T(8,128)(2,1)S(1)}, bf16[2048,512]{1,0:T(8,128)(2,1)S(1)}, u32[]{:S(2)}, u32[]{:S(2)}) %collective-permute-start.9) | collective-permute-done | bytes 2097184 | tf_op jit(solution)/shard_map/ppermute | solution.py:92
  256.6 4.8 constant_dynamic-slice_fusion.16
  270.1 18.5 %bitcast_convert_fusion = bf16[8,576,1024]{2,1,0:T(8,128)(2,1)} fusion(bf16[1,8,576,512]{3,2,1,0:T(8,128)(2,1)} %bitcast.247, bf16[1,8,576,512]{3,2,1,0:T(8,128)(2,1)} %bitcast.246, bf16[8,2,1024,512]{3,2,1,0:T(8,128)(2,1)} %param.22), kind=kOutput, calls=%fused_computation | convolution fusion | flops 9673113600 | bytes 35651584 | tf_op jit(solution)/shard_map/tecf,etdf->ecd/dot_general | solution.py:273
  288.6 5.1 collective-permute-done.12
  294.1 4.9 add_convert_fusion.1
  305.2 5.9 bitcast_convert_fusion.1
  320.8 17.1 %collective-permute-done.16 = bf16[512,512]{1,0:T(8,128)(2,1)S(1)} collective-permute-done((bf16[512,512]{1,0:T(8,128)(2,1)S(1)}, bf16[512,512]{1,0:T(8,128)(2,1)S(1)}, u32[]{:S(2)}, u32[]{:S(2)}) %collective-permute-start.16) | collective-permute-done | bytes 524320 | tf_op jit(solution)/shard_map/ppermute | solution.py:92
  340.1 11.9 %collective-permute-done.15 = bf16[2048,512]{1,0:T(8,128)(2,1)S(1)} collective-permute-done((bf16[2048,512]{1,0:T(8,128)(2,1)S(1)}, bf16[2048,512]{1,0:T(8,128)(2,1)S(1)}, u32[]{:S(2)}, u32[]{:S(2)}) %collective-permute-start.15) | collective-permute-done | bytes 2097184 | tf_op jit(solution)/shard_map/ppermute | solution.py:92
  361.6 9.7 %fusion.78 = bf16[8,64,512]{2,1,0:T(8,128)(2,1)} fusion(bf16[512,8,2,64]{0,3,2,1:T(8,128)(2,1)} %bitcast.198, f32[1,8,2,512,512]{3,4,2,1,0:T(8,128)} %get-tuple-element.158, f32[8,2,512]{2,1,0:T(2,128)S(1)} %bitcast.232), kind=kOutput, calls=%fused_computation.127 | convolution fusion | flops 545521664 | bytes 18382848 | tf_op jit(solution)/shard_map/sgjqk,sqgjd->skgd/dot_general | solution.py:347
  371.3 16.4 %fusion = (f32[8,2,512]{2,1,0:T(2,128)}, f32[8,512,512,2]{2,1,3,0:T(8,128)}) fusion(f32[1,8,2,512,512]{3,4,2,1,0:T(8,128)} %get-tuple-element.158, f32[8,2,512]{2,1,0:T(2,128)} %bitcast.230, bf16[512,8,64,1]{0,2,3,1:T(8,128)(2,1)} %bitcast.229, bf16[512,8,2,64]{0,3,2,1:T(8,128)(2,1)} %bitcast.199), kind=kOutput, calls=%fused_computation.4 | convolution fusion | flops 549445632 | bytes 35192832 | tf_op jit(solution)/shard_map/sqgjd,skgd->sgjqk/dot_general | solution.py:350
  393.4 11.1 %fusion.2 = bf16[1,8,2,512,512]{3,4,2,1,0:T(8,128)(2,1)} fusion(f32[8,512,512,2]{2,1,3,0:T(8,128)} %get-tuple-element.166, f32[1,8,2,512,512]{3,4,2,1,0:T(8,128)S(1)} %bitcast.192, f32[8,2,512]{2,1,0:T(2,128)} %get-tuple-element.165, f32[8,2,512]{2,1,0:T(2,128)} %bitcast.231), kind=kLoop, calls=%fused_computation.6 | loop fusion | flops 16777216 | bytes 42008576 | tf_op jit(solution)/shard_map/convert_element_type | solution.py:355
  411.5 10.1 %collective-permute-done.19 = bf16[512,512]{1,0:T(8,128)(2,1)S(1)} collective-permute-done((bf16[512,512]{1,0:T(8,128)(2,1)S(1)}, bf16[512,512]{1,0:T(8,128)(2,1)S(1)}, u32[]{:S(2)}, u32[]{:S(2)}) %collective-permute-start.19) | collective-permute-done | bytes 524320 | tf_op jit(solution)/shard_map/ppermute | solution.py:92
  435.3 16.2 %collective-permute-done.20 = bf16[512,512]{1,0:T(8,128)(2,1)S(1)} collective-permute-done((bf16[512,512]{1,0:T(8,128)(2,1)S(1)}, bf16[512,512]{1,0:T(8,128)(2,1)S(1)}, u32[]{:S(2)}, u32[]{:S(2)}) %collective-permute-start.20) | collective-permute-done | bytes 524320 | tf_op jit(solution)/shard_map/ppermute | solution.py:92
  451.6 13.9 %collective-permute-done.21 = bf16[1024,512]{1,0:T(8,128)(2,1)S(1)} collective-permute-done((bf16[1024,512]{1,0:T(8,128)(2,1)S(1)}, bf16[1024,512]{1,0:T(8,128)(2,1)S(1)}, u32[]{:S(2)}, u32[]{:S(2)}) %collective-permute-start.21) | collective-permute-done | bytes 1048608 | tf_op jit(solution)/shard_map/ppermute | solution.py:92
  466.8 18.6 %collective-permute-done.22 = bf16[1024,512]{1,0:T(8,128)(2,1)S(1)} collective-permute-done((bf16[1024,512]{1,0:T(8,128)(2,1)S(1)}, bf16[1024,512]{1,0:T(8,128)(2,1)S(1)}, u32[]{:S(2)}, u32[]{:S(2)}) %collective-permute-start.22) | collective-permute-done | bytes 1048608 | tf_op jit(solution)/shard_map/ppermute | solution.py:92
  496.6 11.0 %concatenate.68 = bf16[1024,3200]{1,0:T(8,128)(2,1)} concatenate(bf16[1024,2048]{1,0:T(8,128)(2,1)} %convolution_convert_fusion.8, bf16[1024,1024]{1,0:T(8,128)(2,1)} %convolution_convert_fusion.9, bf16[1024,16]{1,0:T(8,128)(2,1)S(1)} %copy-done.39, bf16[1024,1]{1,0:T(8,128)(2,1)S(1)} %convert_element_type.536, bf16[1024,1]{1,0:T(8,128)(2,1)S(1)} %copy-done.40, ...), dimensions={1} | concatenate | bytes 13107200 | tf_op jit(solution)/shard_map/concatenate | solution.py:397
  512.9 6.0 bitcast_convert_fusion.2
  519.4 85.1 %collective-permute-done.6 = bf16[512,1024]{1,0:T(8,128)(2,1)} collective-permute-done((bf16[512,1024]{1,0:T(8,128)(2,1)}, bf16[512,1024]{1,0:T(8,128)(2,1)}, u32[]{:S(2)}, u32[]{:S(2)}) %collective-permute-start.6) | collective-permute-done | bytes 1048608 | tf_op jit(solution)/shard_map/ppermute | solution.py:66
  604.5 6.2 fusion.52
  620.9 23.8 %collective-permute-done.32 = bf16[512,512]{1,0:T(8,128)(2,1)S(1)} collective-permute-done((bf16[512,512]{1,0:T(8,128)(2,1)S(1)}, bf16[512,512]{1,0:T(8,128)(2,1)S(1)}, u32[]{:S(2)}, u32[]{:S(2)}) %collective-permute-start.32) | collective-permute-done | bytes 524320 | tf_op jit(solution)/shard_map/ppermute | solution.py:92
  647.9 8.0 collective-permute-done.36
  658.4 23.8 %collective-permute-done.37 = bf16[512,512]{1,0:T(8,128)(2,1)S(1)} collective-permute-done((bf16[512,512]{1,0:T(8,128)(2,1)S(1)}, bf16[512,512]{1,0:T(8,128)(2,1)S(1)}, u32[]{:S(2)}, u32[]{:S(2)}) %collective-permute-start.37) | collective-permute-done | bytes 524320 | tf_op jit(solution)/shard_map/ppermute | solution.py:92
  682.5 7.1 collective-permute-done.33
  701.0 4.9 convert_dynamic-update-slice_fusion.5
  705.9 49.0 %collective-permute-done.25 = bf16[128,3200]{1,0:T(8,128)(2,1)} collective-permute-done((bf16[128,3200]{1,0:T(8,128)(2,1)}, bf16[128,3200]{1,0:T(8,128)(2,1)}, u32[]{:S(2)}, u32[]{:S(2)}) %collective-permute-start.25) | collective-permute-done | bytes 819232 | tf_op jit(solution)/shard_map/ppermute | solution.py:92
  770.6 6.8 collective-permute-done.27
  777.6 26.8 %collective-permute-done.39 = bf16[2048,512]{1,0:T(8,128)(2,1)S(1)} collective-permute-done((bf16[2048,512]{1,0:T(8,128)(2,1)S(1)}, bf16[2048,512]{1,0:T(8,128)(2,1)S(1)}, u32[]{:S(2)}, u32[]{:S(2)}) %collective-permute-start.39) | collective-permute-done | bytes 2097184 | tf_op jit(solution)/shard_map/ppermute | solution.py:92
  807.7 11.5 %broadcast_in_dim.152 = f32[8,2,1024,512]{3,2,1,0:T(8,128)} broadcast(f32[]{:T(128)} %constant.31.clone.1), dimensions={} | broadcast | bytes 33554436 | tf_op jit(solution)/shard_map/broadcast_in_dim | solution.py:430
  819.2 6.8 convert_dynamic-update-slice_fusion.3
  830.6 6.6 dynamic_update_slice.135
  839.0 6.8 convert_dynamic-update-slice_fusion.4
  846.1 11.6 %collective-permute-done.30 = bf16[128,3200]{0,1:T(8,128)(2,1)S(1)} collective-permute-done((bf16[128,3200]{0,1:T(8,128)(2,1)S(1)}, bf16[128,3200]{0,1:T(8,128)(2,1)S(1)}, u32[]{:S(2)}, u32[]{:S(2)}) %collective-permute-start.30) | collective-permute-done | bytes 819232 | tf_op jit(solution)/shard_map/ppermute | solution.py:92
  858.4 6.8 convert_dynamic-update-slice_fusion.2
  865.2 6.8 convert_dynamic-update-slice_fusion.1
  872.0 6.8 convert_dynamic-update-slice_fusion
  (427 shorter events, 223.0 us)
Async XLA Ops:
  9.4 28.1 %collective-permute-start = (bf16[256,2176]{1,0:T(8,128)(2,1)}, bf16[256,2176]{1,0:T(8,128)(2,1)}, u32[]{:S(2)}, u32[]{:S(2)}) collective-permute-start(bf16[256,2176]{1,0:T(8,128)(2,1)} %constant_dynamic-slice_fusion.24), channel_id=1, source_target_pairs={{0,16},{16,0},{1,17},{17,1},{2,18},{18,2},{3,19},{19,3},{4,20},{20... | collective-permute-start | bytes 3342344 | tf_op jit(solution)/shard_map/ppermute | solution.py:66
  12.4 25.1 %collective-permute-start.4 = (s32[512,8]{0,1:T(8,128)S(1)}, s32[512,8]{0,1:T(8,128)S(1)}, u32[]{:S(2)}, u32[]{:S(2)}) collective-permute-start(s32[512,8]{0,1:T(8,128)S(1)} %copy-done.68), channel_id=1, source_target_pairs={{0,16},{16,0},{1,17},{17,1},{2,18},{18,2},{3,19},{19,3},{4,20},{20... | collective-permute-start | bytes 49160 | tf_op jit(solution)/shard_map/ppermute | solution.py:66
  20.6 72.7 %copy-start.53 = (s32[8,512]{1,0:T(8,128)}, s32[8,512]{1,0:T(8,128)S(1)}, u32[]{:S(2)}) copy-start(s32[8,512]{1,0:T(8,128)S(1)} %fusion.104) | copy-start | bytes 49156
  37.5 12.0 %collective-permute-start.1 = (bf16[256,2176]{1,0:T(8,128)(2,1)}, bf16[256,2176]{1,0:T(8,128)(2,1)S(1)}, u32[]{:S(2)}, u32[]{:S(2)}) collective-permute-start(bf16[256,2176]{1,0:T(8,128)(2,1)} %collective-permute-done), channel_id=1, source_target_pairs={{0,1},{1,0},{2,3},{3,2},{4,5},{5,4},{6,7},{7,6},{8,9},{9,8},{10,11... | collective-permute-start | bytes 3342344 | tf_op jit(solution)/shard_map/ppermute | solution.py:85
  37.8 267.3 %copy-start.55 = (s32[8,512]{1,0:T(8,128)}, s32[8,512]{1,0:T(8,128)S(1)}, u32[]{:S(2)}) copy-start(s32[8,512]{1,0:T(8,128)S(1)} %fusion.107) | copy-start | bytes 49156
  58.0 19.9 %collective-permute-start.2 = (bf16[256,1024]{1,0:T(8,128)(2,1)S(1)}, bf16[256,1024]{1,0:T(8,128)(2,1)S(1)}, u32[]{:S(2)}, u32[]{:S(2)}) collective-permute-start(bf16[256,1024]{1,0:T(8,128)(2,1)S(1)} %constant_dynamic-slice_fusion.23), channel_id=1, source_target_pairs={{0,16},{16,0},{1,17},{17,1},{2,18},{18,2},{3,19},{19,3},{4,20},{20... | collective-permute-start | bytes 1572872 | tf_op jit(solution)/shard_map/ppermute | solution.py:66
  77.8 8.9 collective-permute-start.3
  89.8 26.1 %collective-permute-start.5 = (bf16[512,1024]{1,0:T(8,128)(2,1)S(1)}, bf16[512,1024]{1,0:T(8,128)(2,1)S(1)}, u32[]{:S(2)}, u32[]{:S(2)}) collective-permute-start(bf16[512,1024]{1,0:T(8,128)(2,1)S(1)} %multiply_convert_fusion.4), channel_id=1, source_target_pairs={{0,16},{16,0},{1,17},{17,1},{2,18},{18,2},{3,19},{19,3},{4,20},{20... | collective-permute-start | bytes 3145736 | tf_op jit(solution)/shard_map/ppermute | solution.py:66
  91.4 50.1 %collective-permute-start.7 = (bf16[512,1024]{1,0:T(8,128)(2,1)S(1)}, bf16[512,1024]{1,0:T(8,128)(2,1)S(1)}, u32[]{:S(2)}, u32[]{:S(2)}) collective-permute-start(bf16[512,1024]{1,0:T(8,128)(2,1)S(1)} %copy-done.37), channel_id=1, source_target_pairs={{0,16},{16,0},{1,17},{17,1},{2,18},{18,2},{3,19},{19,3},{4,20},{20... | collective-permute-start | bytes 3145736 | tf_op jit(solution)/shard_map/ppermute | solution.py:66
  169.9 33.1 %collective-permute-start.8 = (bf16[4096,512]{1,0:T(8,128)(2,1)}, bf16[4096,512]{1,0:T(8,128)(2,1)}, u32[]{:S(2)}, u32[]{:S(2)}) collective-permute-start(bf16[4096,512]{1,0:T(8,128)(2,1)} %constant_dynamic-slice_fusion.18), channel_id=1, source_target_pairs={{0,1},{1,0},{2,3},{3,2},{4,5},{5,4},{6,7},{7,6},{8,9},{9,8},{10,11... | collective-permute-start | bytes 12582920 | tf_op jit(solution)/shard_map/ppermute | solution.py:92
  207.8 48.1 %collective-permute-start.9 = (bf16[2048,512]{1,0:T(8,128)(2,1)S(1)}, bf16[2048,512]{1,0:T(8,128)(2,1)S(1)}, u32[]{:S(2)}, u32[]{:S(2)}) collective-permute-start(bf16[2048,512]{1,0:T(8,128)(2,1)S(1)} %constant_dynamic-slice_fusion.17), channel_id=1, source_target_pairs={{0,2},{1,3},{2,0},{3,1},{4,6},{5,7},{6,4},{7,5},{8,10},{9,11},{10,... | collective-permute-start | bytes 6291464 | tf_op jit(solution)/shard_map/ppermute | solution.py:92
  261.4 32.7 %collective-permute-start.10 = (bf16[4096,512]{1,0:T(8,128)(2,1)}, bf16[4096,512]{1,0:T(8,128)(2,1)}, u32[]{:S(2)}, u32[]{:S(2)}) collective-permute-start(bf16[4096,512]{1,0:T(8,128)(2,1)} %constant_dynamic-slice_fusion.16), channel_id=1, source_target_pairs={{0,1},{1,0},{2,3},{3,2},{4,5},{5,4},{6,7},{7,6},{8,9},{9,8},{10,11... | collective-permute-start | bytes 12582920 | tf_op jit(solution)/shard_map/ppermute | solution.py:92
  262.6 4.2 collective-permute-start.14
  266.5 32.5 %collective-permute-start.11 = (bf16[4096,512]{1,0:T(8,128)(2,1)}, bf16[4096,512]{1,0:T(8,128)(2,1)}, u32[]{:S(2)}, u32[]{:S(2)}) collective-permute-start(bf16[4096,512]{1,0:T(8,128)(2,1)} %constant_dynamic-slice_fusion.15), channel_id=1, source_target_pairs={{0,1},{1,0},{2,3},{3,2},{4,5},{5,4},{6,7},{7,6},{8,9},{9,8},{10,11... | collective-permute-start | bytes 12582920 | tf_op jit(solution)/shard_map/ppermute | solution.py:92
  268.3 25.5 %collective-permute-start.12 = (bf16[1024,512]{1,0:T(8,128)(2,1)S(1)}, bf16[1024,512]{1,0:T(8,128)(2,1)S(1)}, u32[]{:S(2)}, u32[]{:S(2)}) collective-permute-start(bf16[1024,512]{1,0:T(8,128)(2,1)S(1)} %constant_dynamic-slice_fusion.14), channel_id=1, source_target_pairs={{0,4},{1,5},{2,6},{3,7},{4,0},{5,1},{6,2},{7,3},{8,12},{9,13},{10,... | collective-permute-start | bytes 3145736 | tf_op jit(solution)/shard_map/ppermute | solution.py:92
  303.4 48.6 %collective-permute-start.15 = (bf16[2048,512]{1,0:T(8,128)(2,1)S(1)}, bf16[2048,512]{1,0:T(8,128)(2,1)S(1)}, u32[]{:S(2)}, u32[]{:S(2)}) collective-permute-start(bf16[2048,512]{1,0:T(8,128)(2,1)S(1)} %constant_dynamic-slice_fusion.13), channel_id=1, source_target_pairs={{0,2},{1,3},{2,0},{3,1},{4,6},{5,7},{6,4},{7,5},{8,10},{9,11},{10,... | collective-permute-start | bytes 6291464 | tf_op jit(solution)/shard_map/ppermute | solution.py:92
  311.1 27.0 %collective-permute-start.13 = (bf16[512,1024]{1,0:T(8,128)(2,1)S(1)}, bf16[512,1024]{1,0:T(8,128)(2,1)S(1)}, u32[]{:S(2)}, u32[]{:S(2)}) collective-permute-start(bf16[512,1024]{1,0:T(8,128)(2,1)S(1)} %bitcast_convert_fusion.1), channel_id=1, source_target_pairs={{0,16},{16,0},{1,17},{17,1},{2,18},{18,2},{3,19},{19,3},{4,20},{20... | collective-permute-start | bytes 3145736 | tf_op jit(solution)/shard_map/ppermute | solution.py:66
  312.8 25.1 %collective-permute-start.16 = (bf16[512,512]{1,0:T(8,128)(2,1)S(1)}, bf16[512,512]{1,0:T(8,128)(2,1)S(1)}, u32[]{:S(2)}, u32[]{:S(2)}) collective-permute-start(bf16[512,512]{1,0:T(8,128)(2,1)S(1)} %constant_dynamic-slice_fusion.12), channel_id=1, source_target_pairs={{0,8},{1,9},{2,10},{3,11},{4,12},{5,13},{6,14},{7,15},{8,0},{9,1},... | collective-permute-start | bytes 1572872 | tf_op jit(solution)/shard_map/ppermute | solution.py:92
  316.9 91.3 %collective-permute-start.17 = (bf16[2048,512]{1,0:T(8,128)(2,1)}, bf16[2048,512]{1,0:T(8,128)(2,1)}, u32[]{:S(2)}, u32[]{:S(2)}) collective-permute-start(bf16[2048,512]{1,0:T(8,128)(2,1)} %constant_dynamic-slice_fusion.11), channel_id=1, source_target_pairs={{0,2},{1,3},{2,0},{3,1},{4,6},{5,7},{6,4},{7,5},{8,10},{9,11},{10,... | collective-permute-start | bytes 6291464 | tf_op jit(solution)/shard_map/ppermute | solution.py:92
  389.0 33.5 %collective-permute-start.18 = (bf16[1024,512]{1,0:T(8,128)(2,1)S(1)}, bf16[1024,512]{1,0:T(8,128)(2,1)S(1)}, u32[]{:S(2)}, u32[]{:S(2)}) collective-permute-start(bf16[1024,512]{1,0:T(8,128)(2,1)S(1)} %constant_dynamic-slice_fusion.10), channel_id=1, source_target_pairs={{0,4},{1,5},{2,6},{3,7},{4,0},{5,1},{6,2},{7,3},{8,12},{9,13},{10,... | collective-permute-start | bytes 3145736 | tf_op jit(solution)/shard_map/ppermute | solution.py:92
  390.8 30.8 %collective-permute-start.19 = (bf16[512,512]{1,0:T(8,128)(2,1)S(1)}, bf16[512,512]{1,0:T(8,128)(2,1)S(1)}, u32[]{:S(2)}, u32[]{:S(2)}) collective-permute-start(bf16[512,512]{1,0:T(8,128)(2,1)S(1)} %add_convert_fusion.15), channel_id=1, source_target_pairs={{0,8},{1,9},{2,10},{3,11},{4,12},{5,13},{6,14},{7,15},{8,0},{9,1},... | collective-permute-start | bytes 1572872 | tf_op jit(solution)/shard_map/ppermute | solution.py:92
  427.5 24.0 %collective-permute-start.20 = (bf16[512,512]{1,0:T(8,128)(2,1)S(1)}, bf16[512,512]{1,0:T(8,128)(2,1)S(1)}, u32[]{:S(2)}, u32[]{:S(2)}) collective-permute-start(bf16[512,512]{1,0:T(8,128)(2,1)S(1)} %constant_dynamic-slice_fusion.9), channel_id=1, source_target_pairs={{0,8},{1,9},{2,10},{3,11},{4,12},{5,13},{6,14},{7,15},{8,0},{9,1},... | collective-permute-start | bytes 1572872 | tf_op jit(solution)/shard_map/ppermute | solution.py:92
  430.1 35.4 %collective-permute-start.21 = (bf16[1024,512]{1,0:T(8,128)(2,1)S(1)}, bf16[1024,512]{1,0:T(8,128)(2,1)S(1)}, u32[]{:S(2)}, u32[]{:S(2)}) collective-permute-start(bf16[1024,512]{1,0:T(8,128)(2,1)S(1)} %constant_dynamic-slice_fusion.8), channel_id=1, source_target_pairs={{0,4},{1,5},{2,6},{3,7},{4,0},{5,1},{6,2},{7,3},{8,12},{9,13},{10,... | collective-permute-start | bytes 3145736 | tf_op jit(solution)/shard_map/ppermute | solution.py:92
  431.8 53.6 %collective-permute-start.22 = (bf16[1024,512]{1,0:T(8,128)(2,1)S(1)}, bf16[1024,512]{1,0:T(8,128)(2,1)S(1)}, u32[]{:S(2)}, u32[]{:S(2)}) collective-permute-start(bf16[1024,512]{1,0:T(8,128)(2,1)S(1)} %constant_dynamic-update-slice_fusion.22), channel_id=1, source_target_pairs={{0,4},{1,5},{2,6},{3,7},{4,0},{5,1},{6,2},{7,3},{8,12},{9,13},{10,... | collective-permute-start | bytes 3145736 | tf_op jit(solution)/shard_map/ppermute | solution.py:92
  511.4 133.5 %collective-permute-start.23 = (bf16[512,3200]{1,0:T(8,128)(2,1)}, bf16[512,3200]{1,0:T(8,128)(2,1)}, u32[]{:S(2)}, u32[]{:S(2)}) collective-permute-start(bf16[512,3200]{1,0:T(8,128)(2,1)} %constant_dynamic-slice_fusion.7), channel_id=1, source_target_pairs={{0,16},{16,0},{1,17},{17,1},{2,18},{18,2},{3,19},{19,3},{4,20},{20... | collective-permute-start | bytes 9830408 | tf_op jit(solution)/shard_map/ppermute | solution.py:66
  518.9 85.7 %collective-permute-start.6 = (bf16[512,1024]{1,0:T(8,128)(2,1)}, bf16[512,1024]{1,0:T(8,128)(2,1)}, u32[]{:S(2)}, u32[]{:S(2)}) collective-permute-start(bf16[512,1024]{1,0:T(8,128)(2,1)} %bitcast_convert_fusion.2), channel_id=1, source_target_pairs={{0,16},{16,0},{1,17},{17,1},{2,18},{18,2},{3,19},{19,3},{4,20},{20... | collective-permute-start | bytes 3145736 | tf_op jit(solution)/shard_map/ppermute | solution.py:66
  519.4 93.0 %copy-start.22 = (bf16[1024,512]{1,0:T(8,128)(2,1)S(1)}, bf16[1024,512]{1,0:T(8,128)(2,1)}, u32[]{:S(2)}) copy-start(bf16[1024,512]{1,0:T(8,128)(2,1)} %add_convert_fusion.8) | copy-start | bytes 3145732
  519.4 96.2 %copy-start.73 = (f32[512]{0:T(512)S(1)}, f32[512]{0:T(512)}, u32[]{:S(2)}) copy-start(f32[512]{0:T(512)} %get-tuple-element.121) | copy-start | bytes 6148
  610.8 34.0 %collective-permute-start.32 = (bf16[512,512]{1,0:T(8,128)(2,1)S(1)}, bf16[512,512]{1,0:T(8,128)(2,1)S(1)}, u32[]{:S(2)}, u32[]{:S(2)}) collective-permute-start(bf16[512,512]{1,0:T(8,128)(2,1)S(1)} %add_convert_fusion.13), channel_id=1, source_target_pairs={{0,8},{1,9},{2,10},{3,11},{4,12},{5,13},{6,14},{7,15},{8,0},{9,1},... | collective-permute-start | bytes 1572872 | tf_op jit(solution)/shard_map/ppermute | solution.py:92
  612.5 43.4 %collective-permute-start.36 = (bf16[512,512]{1,0:T(8,128)(2,1)S(1)}, bf16[512,512]{1,0:T(8,128)(2,1)S(1)}, u32[]{:S(2)}, u32[]{:S(2)}) collective-permute-start(bf16[512,512]{1,0:T(8,128)(2,1)S(1)} %constant_dynamic-slice_fusion.2), channel_id=1, source_target_pairs={{0,8},{1,9},{2,10},{3,11},{4,12},{5,13},{6,14},{7,15},{8,0},{9,1},... | collective-permute-start | bytes 1572872 | tf_op jit(solution)/shard_map/ppermute | solution.py:92
  614.0 81.2 %collective-permute-start.41 = (bf16[2048,512]{1,0:T(8,128)(2,1)}, bf16[2048,512]{1,0:T(8,128)(2,1)S(1)}, u32[]{:S(2)}, u32[]{:S(2)}) collective-permute-start(bf16[2048,512]{1,0:T(8,128)(2,1)} %constant_dynamic-update-slice_fusion.20), channel_id=1, source_target_pairs={{0,2},{1,3},{2,0},{3,1},{4,6},{5,7},{6,4},{7,5},{8,10},{9,11},{10,... | collective-permute-start | bytes 6291464 | tf_op jit(solution)/shard_map/ppermute | solution.py:92
  644.8 44.8 %collective-permute-start.33 = (bf16[1024,512]{1,0:T(8,128)(2,1)S(1)}, bf16[1024,512]{1,0:T(8,128)(2,1)S(1)}, u32[]{:S(2)}, u32[]{:S(2)}) collective-permute-start(bf16[1024,512]{1,0:T(8,128)(2,1)S(1)} %constant_dynamic-update-slice_fusion.12), channel_id=1, source_target_pairs={{0,4},{1,5},{2,6},{3,7},{4,0},{5,1},{6,2},{7,3},{8,12},{9,13},{10,... | collective-permute-start | bytes 3145736 | tf_op jit(solution)/shard_map/ppermute | solution.py:92
  647.8 48.9 %collective-permute-start.24 = (bf16[256,3200]{1,0:T(8,128)(2,1)S(1)}, bf16[256,3200]{1,0:T(8,128)(2,1)S(1)}, u32[]{:S(2)}, u32[]{:S(2)}) collective-permute-start(bf16[256,3200]{1,0:T(8,128)(2,1)S(1)} %constant_dynamic-slice_fusion.6), channel_id=1, source_target_pairs={{0,1},{1,0},{2,3},{3,2},{4,5},{5,4},{6,7},{7,6},{8,9},{9,8},{10,11... | collective-permute-start | bytes 4915208 | tf_op jit(solution)/shard_map/ppermute | solution.py:92
  656.1 26.0 %collective-permute-start.37 = (bf16[512,512]{1,0:T(8,128)(2,1)S(1)}, bf16[512,512]{1,0:T(8,128)(2,1)S(1)}, u32[]{:S(2)}, u32[]{:S(2)}) collective-permute-start(bf16[512,512]{1,0:T(8,128)(2,1)S(1)} %get-tuple-element.123), channel_id=1, source_target_pairs={{0,8},{1,9},{2,10},{3,11},{4,12},{5,13},{6,14},{7,15},{8,0},{9,1},... | collective-permute-start | bytes 1572872 | tf_op jit(solution)/shard_map/ppermute | solution.py:92
  682.2 74.2 %collective-permute-start.38 = (bf16[1024,512]{1,0:T(8,128)(2,1)S(1)}, bf16[1024,512]{1,0:T(8,128)(2,1)}, u32[]{:S(2)}, u32[]{:S(2)}) collective-permute-start(bf16[1024,512]{1,0:T(8,128)(2,1)S(1)} %constant_dynamic-update-slice_fusion.6), channel_id=1, source_target_pairs={{0,4},{1,5},{2,6},{3,7},{4,0},{5,1},{6,2},{7,3},{8,12},{9,13},{10,... | collective-permute-start | bytes 3145736 | tf_op jit(solution)/shard_map/ppermute | solution.py:92
  689.7 77.8 %collective-permute-start.34 = (bf16[2048,512]{1,0:T(8,128)(2,1)S(1)}, bf16[2048,512]{1,0:T(8,128)(2,1)}, u32[]{:S(2)}, u32[]{:S(2)}) collective-permute-start(bf16[2048,512]{1,0:T(8,128)(2,1)S(1)} %constant_dynamic-update-slice_fusion.10), channel_id=1, source_target_pairs={{0,2},{1,3},{2,0},{3,1},{4,6},{5,7},{6,4},{7,5},{8,10},{9,11},{10,... | collective-permute-start | bytes 6291464 | tf_op jit(solution)/shard_map/ppermute | solution.py:92
  696.7 142.3 %collective-permute-start.42 = (bf16[4096,512]{1,0:T(8,128)(2,1)}, bf16[4096,512]{1,0:T(8,128)(2,1)}, u32[]{:S(2)}, u32[]{:S(2)}) collective-permute-start(bf16[4096,512]{1,0:T(8,128)(2,1)} %constant_dynamic-update-slice_fusion), channel_id=1, source_target_pairs={{0,1},{1,0},{2,3},{3,2},{4,5},{5,4},{6,7},{7,6},{8,9},{9,8},{10,11... | collective-permute-start | bytes 12582920 | tf_op jit(solution)/shard_map/ppermute | solution.py:92
  698.6 56.3 %collective-permute-start.25 = (bf16[128,3200]{1,0:T(8,128)(2,1)}, bf16[128,3200]{1,0:T(8,128)(2,1)}, u32[]{:S(2)}, u32[]{:S(2)}) collective-permute-start(bf16[128,3200]{1,0:T(8,128)(2,1)} %constant_dynamic-slice_fusion.5), channel_id=1, source_target_pairs={{0,2},{1,3},{2,0},{3,1},{4,6},{5,7},{6,4},{7,5},{8,10},{9,11},{10,... | collective-permute-start | bytes 2457608 | tf_op jit(solution)/shard_map/ppermute | solution.py:92
  705.9 100.0 %copy-start.2 = (f32[8192,512]{1,0:T(8,128)}, f32[8192,512]{1,0:T(8,128)S(1)}, u32[]{:S(2)}) copy-start(f32[8192,512]{1,0:T(8,128)S(1)} %convert_dynamic-update-slice_fusion.5) | copy-start | bytes 50331652
  756.3 10.5 %collective-permute-start.26 = (bf16[64,3200]{1,0:T(8,128)(2,1)S(1)}, bf16[64,3200]{1,0:T(8,128)(2,1)S(1)}, u32[]{:S(2)}, u32[]{:S(2)}) collective-permute-start(bf16[64,3200]{1,0:T(8,128)(2,1)S(1)} %constant_dynamic-slice_fusion.4), channel_id=1, source_target_pairs={{0,4},{1,5},{2,6},{3,7},{4,0},{5,1},{6,2},{7,3},{8,12},{9,13},{10,... | collective-permute-start | bytes 1228808 | tf_op jit(solution)/shard_map/ppermute | solution.py:92
  757.7 46.7 %collective-permute-start.39 = (bf16[2048,512]{1,0:T(8,128)(2,1)S(1)}, bf16[2048,512]{1,0:T(8,128)(2,1)S(1)}, u32[]{:S(2)}, u32[]{:S(2)}) collective-permute-start(bf16[2048,512]{1,0:T(8,128)(2,1)S(1)} %constant_dynamic-update-slice_fusion.4), channel_id=1, source_target_pairs={{0,2},{1,3},{2,0},{3,1},{4,6},{5,7},{6,4},{7,5},{8,10},{9,11},{10,... | collective-permute-start | bytes 6291464 | tf_op jit(solution)/shard_map/ppermute | solution.py:92
  766.9 10.5 %collective-permute-start.27 = (bf16[32,3200]{1,0:T(8,128)(2,1)S(1)}, bf16[32,3200]{1,0:T(8,128)(2,1)S(1)}, u32[]{:S(2)}, u32[]{:S(2)}) collective-permute-start(bf16[32,3200]{1,0:T(8,128)(2,1)S(1)} %constant_dynamic-slice_fusion.3), channel_id=1, source_target_pairs={{0,8},{1,9},{2,10},{3,11},{4,12},{5,13},{6,14},{7,15},{8,0},{9,1},... | collective-permute-start | bytes 614408 | tf_op jit(solution)/shard_map/ppermute | solution.py:92
  770.6 87.8 %collective-permute-start.35 = (bf16[4096,512]{1,0:T(8,128)(2,1)}, bf16[4096,512]{1,0:T(8,128)(2,1)}, u32[]{:S(2)}, u32[]{:S(2)}) collective-permute-start(bf16[4096,512]{1,0:T(8,128)(2,1)} %constant_dynamic-update-slice_fusion.8), channel_id=1, source_target_pairs={{0,1},{1,0},{2,3},{3,2},{4,5},{5,4},{6,7},{7,6},{8,9},{9,8},{10,11... | collective-permute-start | bytes 12582920 | tf_op jit(solution)/shard_map/ppermute | solution.py:92
  777.5 28.4 %collective-permute-start.28 = (bf16[32,3200]{1,0:T(8,128)(2,1)S(1)}, bf16[32,3200]{1,0:T(8,128)(2,1)S(1)}, u32[]{:S(2)}, u32[]{:S(2)}) collective-permute-start(bf16[32,3200]{1,0:T(8,128)(2,1)S(1)} %get-tuple-element.125), channel_id=1, source_target_pairs={{0,8},{1,9},{2,10},{3,11},{4,12},{5,13},{6,14},{7,15},{8,0},{9,1},... | collective-permute-start | bytes 614408 | tf_op jit(solution)/shard_map/ppermute | solution.py:92
  805.9 66.1 %collective-permute-start.40 = (bf16[4096,512]{1,0:T(8,128)(2,1)}, bf16[4096,512]{1,0:T(8,128)(2,1)}, u32[]{:S(2)}, u32[]{:S(2)}) collective-permute-start(bf16[4096,512]{1,0:T(8,128)(2,1)} %constant_dynamic-update-slice_fusion.2), channel_id=1, source_target_pairs={{0,1},{1,0},{2,3},{3,2},{4,5},{5,4},{6,7},{7,6},{8,9},{9,8},{10,11... | collective-permute-start | bytes 12582920 | tf_op jit(solution)/shard_map/ppermute | solution.py:92
  805.9 24.3 %collective-permute-start.29 = (bf16[64,3200]{1,0:T(8,128)(2,1)S(1)}, bf16[64,3200]{1,0:T(8,128)(2,1)S(1)}, u32[]{:S(2)}, u32[]{:S(2)}) collective-permute-start(bf16[64,3200]{1,0:T(8,128)(2,1)S(1)} %constant_dynamic-update-slice_fusion.18), channel_id=1, source_target_pairs={{0,4},{1,5},{2,6},{3,7},{4,0},{5,1},{6,2},{7,3},{8,12},{9,13},{10,... | collective-permute-start | bytes 1228808 | tf_op jit(solution)/shard_map/ppermute | solution.py:92
  837.3 20.4 %collective-permute-start.30 = (bf16[128,3200]{0,1:T(8,128)(2,1)S(1)}, bf16[128,3200]{0,1:T(8,128)(2,1)S(1)}, u32[]{:S(2)}, u32[]{:S(2)}) collective-permute-start(bf16[128,3200]{0,1:T(8,128)(2,1)S(1)} %dynamic_update_slice.135), channel_id=1, source_target_pairs={{0,2},{1,3},{2,0},{3,1},{4,6},{5,7},{6,4},{7,5},{8,10},{9,11},{10,... | collective-permute-start | bytes 2457608 | tf_op jit(solution)/shard_map/ppermute | solution.py:92
  857.9 20.8 %collective-permute-start.31 = (bf16[256,3200]{0,1:T(8,128)(2,1)S(1)}, bf16[256,3200]{0,1:T(8,128)(2,1)S(1)}, u32[]{:S(2)}, u32[]{:S(2)}) collective-permute-start(bf16[256,3200]{0,1:T(8,128)(2,1)S(1)} %constant_dynamic-update-slice_fusion.16), channel_id=1, source_target_pairs={{0,1},{1,0},{2,3},{3,2},{4,5},{5,4},{6,7},{7,6},{8,9},{9,8},{10,11... | collective-permute-start | bytes 4915208 | tf_op jit(solution)/shard_map/ppermute | solution.py:92
  (88 other events, 1235.7 us)
